TPU v7x, 32 devices: a whole 2x2x4 slice. The times are simulated.
32 devices in a mesh: dom: 4 (over y, core), sub: 8 (over z, x).
Axes of the slice: x: 2, y: 2, z: 4, core: 2. Of those that a mesh axis runs over, the one named last changes fastest.
Arguments:
- node_feat: bfloat16 [304, 16384], P(None, ('dom', 'sub')), may hold values from -6 to 6
- node_pos: bfloat16 [3, 16384], P(None, ('dom', 'sub')), may hold values from -4 to 4
- node_cot: bfloat16 [304, 16384], P(None, ('dom', 'sub')), may hold values from -6 to 6
- mesh_senders: int32 [98304], P(('dom', 'sub')), may hold values from 0 to 1535
- edge_mask: int32 [98304], P(('dom', 'sub')), may hold values 0 or 1
- halo_up: int32 [16384], P(('dom', 'sub')), may hold values from 0 to 511
- halo_down: int32 [16384], P(('dom', 'sub')), may hold values from 0 to 511
- contact_rows: int32 [65536], P(('dom', 'sub')), may hold values from 0 to 511
- contact_dst: int32 [65536], P(('dom', 'sub')), may hold values from 0 to 511
- contact_mask: int32 [65536], P(('dom', 'sub')), may hold values from 0 to 1, as said below
- w_one: bfloat16 [128, 128], replicated, may hold values from -0.5 to 0.5
- b_one: float32 [128], replicated, may hold values from -3 to 3
- w_dist: float32 [128], replicated, may hold values from -3 to 3
- w_two: bfloat16 [144, 128], replicated, may hold values from -0.5 to 0.5
- w_scal: bfloat16 [64, 64], replicated, may hold values from -0.75 to 0.75
- w_vec: bfloat16 [32, 32], replicated, may hold values from -1 to 1
- w_ten: bfloat16 [16, 16], replicated, may hold values from -1.5 to 1.5
Outputs:
- node_out: bfloat16 [304, 16384], P(None, ('dom', 'sub'))
- grad_one: float32 [128, 128], replicated
- grad_bias: float32 [128], replicated
- grad_dist: float32 [128], replicated
- grad_two: float32 [144, 128], replicated
- grad_scal: float32 [64, 64], replicated
- grad_vec: float32 [32, 32], replicated
- grad_ten: float32 [16, 16], replicated
Inputs may be any that keep to these rules, and one draw needn't show every extreme that they name: `mesh_senders`: below 512 an own node, then the block from the previous and the block from the next sub-partition. `contact_rows`: entry p * 2048 + c * 64 + k names a row of partition c. `contact_mask`: in every draw some partition has all 2048 contact slots live; partitions differ in how many are.
All inputs are finite; a program needn't handle non-finite values. No bound on the sum of `edge_mask` on one device may be relied on, other than what follows from the above.
Results may differ from a plain program's by a relative error of at most 0.0059.
Values may be sent and summed in bfloat16 or wider, within the bound.
No kernel may reach another device: no remote copies, remote signals or barrier semaphores. Data moves between devices by JAX's collectives and lax.ppermute only.
A program may use at most 128 MiB of HBM per device.

v0:
```python
import functools
import math

import jax
import jax.numpy as jnp
from jax import lax
from jax.experimental import pallas as pl
from jax.experimental.pallas import tpu as pltpu
from jax.sharding import PartitionSpec as P

CS = 64
CV = 32
CT = 16
HID = 128
DEGREE = 6
GATES = 144
FEAT = CS + 3 * CV + 9 * CT
ROWS = 320
LANES = 128
FINE = 4
CHUNK = 512
WIDE = 1024
VMEM_BYTES = 48 * 1024 * 1024


def dot(lhs, rhs, lhs_dim=1, rhs_dim=0):
    return lax.dot_general(
        lhs, rhs, (((lhs_dim,), (rhs_dim,)), ((), ())), preferred_element_type=jnp.float32
    )


def one_hot(code, width):
    rows = lax.broadcasted_iota(jnp.int16, (width, code.shape[1]), 0)
    return jnp.where(rows == code.astype(jnp.int16), jnp.bfloat16(1), jnp.bfloat16(0))


def join_index(table, row):
    pair = table[row : row + 2].astype(jnp.float32)
    return (pair[0:1] * 128.0 + pair[1:2]).astype(jnp.int32)


def table_kernel(
    feat_ref,
    pos_ref,
    up_ref,
    down_ref,
    rows_ref,
    table_ref,
    request_ref,
    pos_scr,
    up_scr,
    down_scr,
    rows_scr,
    sems,
):
    node_count = table_ref.shape[1]
    copies = [
        pltpu.make_async_copy(rows_ref, rows_scr, sems.at[0]),
        pltpu.make_async_copy(feat_ref, table_ref.at[:FEAT], sems.at[1]),
        pltpu.make_async_copy(pos_ref, pos_scr, sems.at[2]),
        pltpu.make_async_copy(up_ref, up_scr, sems.at[3]),
        pltpu.make_async_copy(down_ref, down_scr, sems.at[4]),
    ]
    for copy in copies:
        copy.start()
    copies[0].wait()
    slot = request_ref.shape[2]
    parts = LANES // slot
    for row in range(rows_scr.shape[0]):
        line = rows_scr[row : row + 1]
        for part in range(parts):
            request_ref[row * parts + part] = line[:, part * slot : (part + 1) * slot]
    for copy in copies[2:]:
        copy.wait()
    rows = lax.broadcasted_iota(jnp.int32, (ROWS - FEAT, node_count), 0)
    pos = pos_scr[...].astype(jnp.float32)
    tail = jnp.zeros((ROWS - FEAT, node_count), jnp.float32)
    for k in range(3):
        tail = jnp.where(rows == k, pos[k : k + 1], tail)
    for k, index_ref in ((3, up_scr), (5, down_scr)):
        index = index_ref[...]
        high = index >> 7
        tail = jnp.where(rows == k, high.astype(jnp.float32), tail)
        tail = jnp.where(rows == k + 1, (index - (high << 7)).astype(jnp.float32), tail)
    table_ref[FEAT:] = tail.astype(jnp.bfloat16)
    copies[1].wait()


def contact_gather_kernel(slot, table_ref, wanted_ref, out_hbm, out_ref, sems):
    node_count = table_ref.shape[1]
    parts = LANES // slot
    height = out_ref.shape[1]
    per_chunk = CHUNK // slot
    copies = []
    for chunk in range(wanted_ref.shape[0] // per_chunk):
        wanted = [wanted_ref[chunk * per_chunk + peer] for peer in range(per_chunk)]
        hot = one_hot(jnp.concatenate(wanted, 1), node_count)
        rows = dot(table_ref[...], hot).astype(jnp.bfloat16)
        if parts * height > ROWS:
            rows = jnp.concatenate(
                [rows, jnp.zeros((parts * height - ROWS, CHUNK), jnp.bfloat16)], 0
            )
        for peer in range(per_chunk):
            out_ref[chunk * per_chunk + peer] = jnp.concatenate(
                [
                    rows[part * height : (part + 1) * height, peer * slot : (peer + 1) * slot]
                    for part in range(parts)
                ],
                1,
            )
        done = pl.ds(chunk * per_chunk, per_chunk)
        copies.append(
            pltpu.make_async_copy(out_ref.at[done], out_hbm.at[done], sems.at[chunk])
        )
        copies[-1].start()
    for copy in copies:
        copy.wait()


def edge_math(src, base, first, inputs, pos_recv, back, live, weights):
    w_dist, w_two, w_two_t = weights
    edges = src.shape[1]
    offset = src[FEAT : FEAT + 3] - pos_recv
    if live is not None:
        offset = offset * live
    distance = jnp.sum(offset * offset, 0, keepdims=True)
    linear = base + first + w_dist * distance
    squashed = 0.5 * jnp.tanh(0.5 * linear) + 0.5
    hidden = (linear * squashed).astype(jnp.bfloat16)
    gates = dot(w_two, hidden)
    gate_vec = gates[CS : CS + CV]
    gate_dir = gates[CS + CV : CS + 2 * CV]
    gate_ten = gates[CS + 2 * CV :]
    message = [gates[:CS] * src[:CS]]
    vec_part = jnp.zeros((CV, edges), jnp.float32)
    dir_part = jnp.zeros((CV, edges), jnp.float32)
    for k in range(3):
        rows = slice(CS + k * CV, CS + (k + 1) * CV)
        message.append(gate_vec * src[rows] + gate_dir * offset[k : k + 1])
        vec_part = vec_part + back[rows] * src[rows]
        dir_part = dir_part + back[rows] * offset[k : k + 1]
    ten_part = jnp.zeros((CT, edges), jnp.float32)
    for m in range(9):
        rows = slice(CS + 3 * CV + m * CT, CS + 3 * CV + (m + 1) * CT)
        message.append(gate_ten * src[rows])
        ten_part = ten_part + back[rows] * src[rows]
    message = jnp.concatenate(message, 0)
    dgates = jnp.concatenate([back[:CS] * src[:CS], vec_part, dir_part, ten_part], 0).astype(
        jnp.bfloat16
    )
    hidden_grad = dot(w_two_t, dgates)
    linear_grad = (hidden_grad * squashed * (1.0 + linear * (1.0 - squashed))).astype(jnp.bfloat16)
    rows = lax.broadcasted_iota(jnp.int32, (16, edges), 0)
    coarse = distance.astype(jnp.bfloat16).astype(jnp.float32)
    extra = jnp.where(
        rows == 0, 1.0, jnp.where(rows == 1, coarse, jnp.where(rows == 2, distance - coarse, 0.0))
    ).astype(jnp.bfloat16)
    grads = (
        dot(linear_grad, jnp.concatenate([inputs, extra], 0), 1, 1),
        dot(dgates, hidden, 1, 1),
    )
    return message, grads


def as_columns(first_row, second_row):
    rows = lax.broadcasted_iota(jnp.int32, (LANES, LANES), 0)
    columns = jnp.where(rows == 0, first_row, jnp.where(rows == 1, second_row, 0.0)).T
    return columns[:, 0:1], columns[:, 1:2]


def add_grads(grads_ref, grads):
    grads_ref[:HID, : 2 * CS + 16] += grads[0]
    grads_ref[HID:, :HID] += grads[1]


def block_diagonal(block_ref, w_scal, w_vec, w_ten):
    block_ref[...] = jnp.zeros_like(block_ref)
    block_ref[:CS, :CS] = w_scal[...]
    for k in range(3):
        rows = slice(CS + k * CV, CS + (k + 1) * CV)
        block_ref[rows, rows] = w_vec[...]
    for m in range(9):
        rows = slice(CS + 3 * CV + m * CT, CS + 3 * CV + (m + 1) * CT)
        block_ref[rows, rows] = w_ten[...]


def mesh_kernel(
    table_ref,
    low_ref,
    high_ref,
    code_ref,
    cot_ref,
    w_one_ref,
    b_one_ref,
    w_dist_ref,
    w_two_ref,
    w_scal_ref,
    w_vec_ref,
    w_ten_ref,
    dst_ref,
    mask_ref,
    agg_out_ref,
    grads_out_ref,
    recv_out_ref,
    code_out_ref,
    agg_ref,
    grads_ref,
    recv_ref,
    receive_ref,
    source_ref,
    block_ref,
    contact_ref,
    sems,
):
    node_count = table_ref.shape[1]
    source_ref[:, :node_count] = table_ref[...]
    low = low_ref[...]
    high = high_ref[...]
    source_ref[:, node_count : 2 * node_count] = dot(
        low, one_hot(join_index(low, FEAT + 3), node_count)
    ).astype(jnp.bfloat16)
    source_ref[:, 2 * node_count :] = dot(
        high, one_hot(join_index(high, FEAT + 5), node_count)
    ).astype(jnp.bfloat16)
    block_diagonal(block_ref, w_scal_ref, w_vec_ref, w_ten_ref)
    receive_ref[:FEAT] = dot(block_ref[...], cot_ref[...], 0, 0).astype(jnp.bfloat16)
    receive_ref[FEAT : FEAT + 16] = table_ref[FEAT:]
    receive_ref[FEAT + 16 :] = table_ref[:CS]
    w_one = w_one_ref[...]
    w_two = w_two_ref[...]
    b_column, dist_column = as_columns(b_one_ref[...], w_dist_ref[...])
    scal_recv = table_ref[:CS]
    recv_linear = dot(w_one[:, :CS], scal_recv) + b_column
    weights = (dist_column, w_two, w_two.T)
    pos_recv = table_ref[FEAT:].astype(jnp.float32)[:3]
    grads_ref[...] = jnp.zeros_like(grads_ref)
    agg_ref[...] = jnp.zeros_like(agg_ref)
    for step in range(DEGREE):
        code = code_ref[step]
        src = dot(source_ref[...], one_hot(code, 3 * node_count))
        live = jnp.where(code >= 0, 1.0, 0.0)
        back = receive_ref[:FEAT].astype(jnp.float32)
        scal_send = src[:CS].astype(jnp.bfloat16)
        inputs = jnp.concatenate([scal_recv, scal_send], 0)
        message, grads = edge_math(
            src, recv_linear, dot(w_one[:, CS:], scal_send), inputs, pos_recv, back, live, weights
        )
        agg_ref[...] += message
        add_grads(grads_ref, grads)
    contact_ref[...] = jnp.where(mask_ref[...] != 0, dst_ref[...], -1)
    for chunk in range(contact_ref.shape[0]):
        recv_ref[chunk] = dot(
            receive_ref[...], one_hot(contact_ref[chunk], node_count)
        ).astype(jnp.bfloat16)
    copies = [
        pltpu.make_async_copy(agg_ref, agg_out_ref, sems.at[0]),
        pltpu.make_async_copy(grads_ref, grads_out_ref, sems.at[1]),
        pltpu.make_async_copy(recv_ref, recv_out_ref, sems.at[2]),
        pltpu.make_async_copy(contact_ref, code_out_ref, sems.at[3]),
    ]
    for copy in copies:
        copy.start()
    for copy in copies:
        copy.wait()


def contact_kernel(
    slot,
    grad_scale,
    reply_ref,
    cot_ref,
    code_hbm,
    recv_hbm,
    mesh_agg_hbm,
    mesh_grads_hbm,
    w_one_hbm,
    w_two_hbm,
    b_one_hbm,
    w_dist_hbm,
    agg_out_ref,
    packed_ref,
    code_ref,
    recv_ref,
    agg_ref,
    grads_ref,
    w_one_ref,
    w_two_ref,
    b_one_ref,
    w_dist_ref,
    src_scr,
    packed_scr,
    sems,
):
    chunks = code_ref.shape[0]
    sources = [
        (b_one_hbm, b_one_ref),
        (w_dist_hbm, w_dist_ref),
        (w_one_hbm, w_one_ref),
        (w_two_hbm, w_two_ref),
        (code_hbm, code_ref),
    ]
    sources += [(recv_hbm.at[chunk], recv_ref.at[chunk]) for chunk in range(chunks)]
    sources += [(mesh_agg_hbm, agg_ref), (mesh_grads_hbm, grads_ref)]
    copies = [
        pltpu.make_async_copy(source, target, sems.at[at])
        for at, (source, target) in enumerate(sources)
    ]
    for copy in copies:
        copy.start()
    node_count = cot_ref.shape[1]
    parts = LANES // slot
    per_chunk = WIDE // slot
    for chunk in range(chunks):
        blocks = [reply_ref[chunk * per_chunk + peer] for peer in range(per_chunk)]
        src_scr[chunk] = jnp.concatenate(
            [
                jnp.concatenate(
                    [block[:, part * slot : (part + 1) * slot] for block in blocks], 1
                )
                for part in range(parts)
            ],
            0,
        )[:ROWS]
    for copy in copies[:6]:
        copy.wait()
    w_one = w_one_ref[...]
    w_two = w_two_ref[...]
    b_column, dist_column = as_columns(b_one_ref[...], w_dist_ref[...])
    weights = (dist_column, w_two, w_two.T)
    for chunk in range(chunks):
        src_rows = src_scr[chunk]
        if chunk == 1:
            for copy in copies[6:]:
                copy.wait()
        recv = recv_ref[chunk]
        inputs = jnp.concatenate([recv[FEAT + 16 :], src_rows[:CS]], 0)
        message, grads = edge_math(
            src_rows.astype(jnp.float32),
            b_column,
            dot(w_one, inputs),
            inputs,
            recv[FEAT : FEAT + 16].astype(jnp.float32)[:3],
            recv[:FEAT].astype(jnp.float32),
            None,
            weights,
        )
        scattered = dot(message.astype(jnp.bfloat16), one_hot(code_ref[chunk], node_count), 1, 1)
        if chunk == 0:
            held = (scattered, grads)
            continue
        agg_ref[...] += scattered
        add_grads(grads_ref, grads)
        if chunk == 1:
            agg_ref[...] += held[0]
            add_grads(grads_ref, held[1])
    agg_rows = agg_ref[...].astype(jnp.bfloat16)
    agg_out_ref[...] = agg_rows
    cot = cot_ref[...]
    low = HID + GATES
    packed_scr[:low] = grads_ref[:, :LANES] * grad_scale
    packed_scr[low : low + CS] = jnp.concatenate(
        [
            dot(cot[:CS], agg_rows[:CS], 1, 1) * grad_scale,
            jnp.zeros((CS, LANES - CS), jnp.float32),
        ],
        1,
    )
    mixed = dot(cot[CS:], agg_rows[CS:], 1, 1)
    grad_vec = jnp.zeros((CV, CV), jnp.float32)
    for k in range(3):
        rows = slice(k * CV, (k + 1) * CV)
        grad_vec = grad_vec + mixed[rows, rows]
    packed_scr[low : low + CV, CS : CS + CV] = grad_vec * grad_scale
    grad_ten = jnp.zeros((CT, CT), jnp.float32)
    for m in range(9):
        rows = slice(3 * CV + m * CT, 3 * CV + (m + 1) * CT)
        grad_ten = grad_ten + mixed[rows, rows]
    packed_scr[low : low + CT, CS + CV : CS + CV + CT] = grad_ten * grad_scale
    extra = (grads_ref[:HID, LANES:] * grad_scale).T[:16]
    rows = lax.broadcasted_iota(jnp.int32, (16, LANES), 0)
    packed_scr[low + CS :] = jnp.where(rows == 1, extra[1:2] + extra[2:3], extra)
    packed = packed_scr[...].astype(jnp.bfloat16)
    tiles = packed_ref.shape[1]
    for peer in range(packed_ref.shape[0]):
        for tile in range(tiles):
            at = (peer * tiles + tile) * FINE
            if at < packed.shape[0]:
                packed_ref[peer, tile] = packed[at : at + FINE]
            else:
                packed_ref[peer, tile] = jnp.zeros((FINE, LANES), jnp.bfloat16)


def sum_kernel(parts_ref, out_ref):
    total = parts_ref[0].astype(jnp.float32)
    for peer in range(1, parts_ref.shape[0]):
        total = total + parts_ref[peer].astype(jnp.float32)
    total = total.astype(jnp.bfloat16)
    for peer in range(out_ref.shape[0]):
        out_ref[peer] = total


def finish_kernel(
    blocks_ref,
    table_ref,
    agg_ref,
    w_scal_ref,
    w_vec_ref,
    w_ten_ref,
    out_ref,
    one_ref,
    bias_ref,
    dist_ref,
    two_ref,
    scal_ref,
    vec_ref,
    ten_ref,
    block_ref,
):
    block_diagonal(block_ref, w_scal_ref, w_vec_ref, w_ten_ref)
    out_ref[...] = (
        table_ref[:FEAT].astype(jnp.float32) + dot(block_ref[...], agg_ref[...])
    ).astype(jnp.bfloat16)

    tiles = blocks_ref.shape[1]

    def rows_of(at):
        peer, tile = divmod(at // FINE, tiles)
        return blocks_ref[peer, tile].astype(jnp.float32)

    for at in range(0, HID, FINE):
        one_ref[at : at + FINE] = rows_of(at)
    for at in range(0, GATES, FINE):
        two_ref[at : at + FINE] = rows_of(HID + at)
    low = HID + GATES
    for at in range(0, CS, FINE):
        rows = rows_of(low + at)
        scal_ref[at : at + FINE] = rows[:, :CS]
        if at < CV:
            vec_ref[at : at + FINE] = rows[:, CS : CS + CV]
        if at < CT:
            ten_ref[at : at + FINE] = rows[:, CS + CV : CS + CV + CT]
    extra = rows_of(low + CS)
    bias_ref[...] = extra[0:1]
    dist_ref[...] = extra[1:2]


def call(kernel, out_shape, scratch=(), in_specs=None, out_specs=None, cost_estimate=None):
    specs = {}
    if cost_estimate is not None:
        specs["cost_estimate"] = cost_estimate
    if in_specs is not None:
        specs["in_specs"] = in_specs
    if out_specs is not None:
        specs["out_specs"] = out_specs
    return pl.pallas_call(
        kernel,
        out_shape=out_shape,
        scratch_shapes=list(scratch),
        compiler_params=pltpu.CompilerParams(vmem_limit_bytes=VMEM_BYTES),
        **specs,
    )


IN_VMEM = pl.BlockSpec(memory_space=pltpu.VMEM)
IN_HBM = pl.BlockSpec(memory_space=pltpu.HBM)
ANYWHERE = pl.BlockSpec(memory_space=pl.ANY)


def exchange(blocks, axes=("dom", "sub")):
    return lax.all_to_all(blocks, axes, split_axis=0, concat_axis=0, tiled=True)


def in_hbm(*arrays):
    return tuple(pltpu.with_memory_space_constraint(array, pltpu.HBM) for array in arrays)


def shaped(shape, dtype):
    return jax.ShapeDtypeStruct(shape, dtype)


def from_behind(shard, axis, by):
    peers = lax.axis_size(axis)
    return lax.ppermute(shard, axis, [(i, (i + by) % peers) for i in range(peers)])


def on_device(
    node_feat,
    node_pos,
    node_cot,
    mesh_senders,
    edge_mask,
    halo_up,
    halo_down,
    contact_rows,
    contact_dst,
    contact_mask,
    w_one,
    b_one,
    w_dist,
    w_two,
    w_scal,
    w_vec,
    w_ten,
):
    f32, bf16 = jnp.float32, jnp.bfloat16
    node_count = node_feat.shape[1]
    contact_count = contact_rows.shape[0]
    device_count = lax.axis_size("dom") * lax.axis_size("sub")
    slot = contact_count // device_count
    chunks = contact_count // CHUNK
    wides = contact_count // WIDE
    parts = LANES // slot
    height = -(-ROWS // (parts * 16)) * 16
    grad_scale = 1.0 / math.sqrt(device_count * node_count * DEGREE)
    table, requests = call(
        table_kernel,
        (
            shaped((ROWS, node_count), bf16),
            shaped((device_count, 1, slot), jnp.int32),
        ),
        (
            pltpu.VMEM((3, node_count), bf16),
            pltpu.VMEM((1, node_count), jnp.int32),
            pltpu.VMEM((1, node_count), jnp.int32),
            pltpu.VMEM((contact_count // LANES, LANES), jnp.int32),
            pltpu.SemaphoreType.DMA((5,)),
        ),
        in_specs=[IN_HBM] * 5,
        out_specs=(IN_VMEM, IN_VMEM),
    )(
        *in_hbm(
            node_feat,
            node_pos,
            halo_up[None],
            halo_down[None],
            contact_rows.reshape(contact_count // LANES, LANES),
        )
    )
    wanted = exchange(requests)
    wanted, table_late = lax.optimization_barrier((wanted, table))
    low = from_behind(table_late, "sub", 1)
    high = from_behind(table_late, "sub", -1)
    found = call(
        functools.partial(contact_gather_kernel, slot),
        pltpu.HBM((device_count, height, LANES), bf16),
        (
            pltpu.VMEM((device_count, height, LANES), bf16),
            pltpu.SemaphoreType.DMA((chunks,)),
        ),
        in_specs=[IN_VMEM, IN_VMEM],
        out_specs=IN_HBM,
    )(table, wanted)
    found, mesh_senders, edge_mask = lax.optimization_barrier((found, mesh_senders, edge_mask))
    replies = exchange(found)
    mesh_code = (
        jnp.where(edge_mask != 0, mesh_senders, -1)
        .reshape(node_count, DEGREE)
        .T.reshape(DEGREE, 1, node_count)
    )
    contact_dst = contact_dst.reshape(wides, 1, WIDE)
    contact_mask = contact_mask.reshape(wides, 1, WIDE)
    mesh_rows = HID + GATES
    recv_rows = FEAT + 16 + CS
    mesh_agg, mesh_grads, recv, contact_code = call(
        mesh_kernel,
        (
            pltpu.HBM((FEAT, node_count), f32),
            pltpu.HBM((mesh_rows, 2 * LANES), f32),
            pltpu.HBM((wides, recv_rows, WIDE), bf16),
            pltpu.HBM((wides, 1, WIDE), jnp.int32),
        ),
        (
            pltpu.VMEM((FEAT, node_count), f32),
            pltpu.VMEM((mesh_rows, 2 * LANES), f32),
            pltpu.VMEM((wides, recv_rows, WIDE), bf16),
            pltpu.VMEM((recv_rows, node_count), bf16),
            pltpu.VMEM((ROWS, 3 * node_count), bf16),
            pltpu.VMEM((FEAT, FEAT), bf16),
            pltpu.VMEM((wides, 1, WIDE), jnp.int32),
            pltpu.SemaphoreType.DMA((4,)),
        ),
        in_specs=[IN_VMEM] * 14,
        out_specs=(IN_HBM,) * 4,
        cost_estimate=pl.CostEstimate(
            flops=40_000_000_000, bytes_accessed=8_000_000, transcendentals=400_000
        ),
    )(
        table,
        low,
        high,
        mesh_code,
        node_cot,
        w_one,
        b_one[None],
        w_dist[None],
        w_two,
        w_scal,
        w_vec,
        w_ten,
        contact_dst,
        contact_mask,
    )
    packed_rows = mesh_rows + CS + 16
    tiles = -(-packed_rows // (FINE * device_count))
    share = (device_count, tiles, FINE, LANES)
    agg_rows, packed = call(
        functools.partial(contact_kernel, slot, grad_scale),
        (shaped((FEAT, node_count), bf16), shaped(share, bf16)),
        (
            pltpu.VMEM((wides, 1, WIDE), jnp.int32),
            pltpu.VMEM((wides, recv_rows, WIDE), bf16),
            pltpu.VMEM((FEAT, node_count), f32),
            pltpu.VMEM((mesh_rows, 2 * LANES), f32),
            pltpu.VMEM((HID, 2 * CS), bf16),
            pltpu.VMEM((GATES, HID), bf16),
            pltpu.VMEM((1, HID), f32),
            pltpu.VMEM((1, HID), f32),
            pltpu.VMEM((wides, ROWS, WIDE), bf16),
            pltpu.VMEM((packed_rows, LANES), f32),
            pltpu.SemaphoreType.DMA((wides + 7,)),
        ),
        in_specs=[IN_VMEM] * 2 + [IN_HBM] * 8,
        out_specs=(IN_VMEM, IN_VMEM),
    )(
        replies,
        node_cot,
        *in_hbm(
            contact_code, recv, mesh_agg, mesh_grads, w_one, w_two, b_one[None], w_dist[None]
        ),
    )
    shares = call(sum_kernel, shaped(share, bf16))(exchange(packed))
    node_out, one, bias, dist, two, scal, vec, ten = call(
        finish_kernel,
        (
            shaped((FEAT, node_count), bf16),
            shaped((HID, 2 * CS), f32),
            shaped((1, HID), f32),
            shaped((1, HID), f32),
            shaped((GATES, HID), f32),
            shaped((CS, CS), f32),
            shaped((CV, CV), f32),
            shaped((CT, CT), f32),
        ),
        (pltpu.VMEM((FEAT, FEAT), bf16),),
    )(exchange(shares), table, agg_rows, w_scal, w_vec, w_ten)
    return node_out, one, bias[0], dist[0], two, scal, vec, ten


def solution(mesh):
    along = P(("dom", "sub"))
    columns = P(None, ("dom", "sub"))
    in_specs = (columns,) * 3 + (along,) * 7 + (P(),) * 7
    out_specs = (columns,) + (P(),) * 7
    return jax.shard_map(
        on_device, mesh=mesh, in_specs=in_specs, out_specs=out_specs, check_vma=False
    )
```

profile of v0, /device:TPU:0, one launch (start us, length us, event | category | flops | bytes accessed | tf_op | source)
XLA Modules:
  0.0 81.0 jit_solution(13206376361929100047)
XLA Ops:
  0.6 1.0 %shard_map.224 = (bf16[320,512]{1,0:T(8,128)(2,1)S(1)}, s32[32,1,64]{2,1,0:T(1,128)S(1)}) custom-call(bf16[304,512]{1,0:T(8,128)(2,1)} %feat_ref.1, bf16[3,512]{1,0:T(4,128)(2,1)} %pos_ref.1, s32[1,512]{1,0:T(1,128)} %bitcast.18, s32[1,512]{1,0:T(1,128)} %bitcast.19, s32[16,128]{1,0:T(8,128)} %bitcast.17), custom_call_target="tpu_custom_call" | custom-call | tf_op jit(solution)/shard_map/pallas_call | solution.py:515
  1.7 14.2 %all_to_all.20.wanted_ref = s32[32,1,64]{2,1,0:T(1,128)S(1)} all-to-all(s32[32,1,64]{2,1,0:T(1,128)S(1)} %get-tuple-element.30), channel_id=1, replica_groups=mesh['dom'=4,'sub'=8] {'dom','sub'}, dimensions={0} | all-to-all | bytes 16384 | tf_op jit(solution)/shard_map/all_to_all | solution.py:470
  15.9 0.6 collective-permute-start.1
  16.5 1.4 %collective-permute-start = (bf16[320,512]{1,0:T(8,128)(2,1)S(1)}, bf16[320,512]{1,0:T(8,128)(2,1)S(1)}, u32[]{:S(2)}, u32[]{:S(2)}) collective-permute-start(bf16[320,512]{1,0:T(8,128)(2,1)S(1)} %get-tuple-element.33.table_ref), channel_id=1, source_target_pairs={{0,1},{1,2},{2,3},{3,4},{4,5},{5,6},{6,7},{7,0},{8,9},{9,10},{10,1... | collective-permute-start | bytes 983048 | tf_op jit(solution)/shard_map/ppermute | solution.py:483
  17.9 1.8 %shard_map.225 = bf16[32,160,128]{2,1,0:T(8,128)(2,1)} custom-call(bf16[320,512]{1,0:T(8,128)(2,1)S(1)} %get-tuple-element.33.table_ref, s32[32,1,64]{2,1,0:T(1,128)S(1)} %all_to_all.20.wanted_ref), custom_call_target="tpu_custom_call" | custom-call | tf_op jit(solution)/shard_map/pallas_call | solution.py:543
  19.7 0.0 copy-start.10
  19.7 0.0 copy-start.11
  19.7 0.0 copy-start
  19.8 0.0 copy-start.1
  19.8 0.0 copy-start.2
  19.8 0.0 copy-start.3
  19.8 0.0 copy-start.4
  19.8 0.0 copy-start.5
  19.8 0.0 copy-start.6
  19.8 0.0 copy-start.7
  19.8 0.0 copy-start.8
  19.8 0.0 copy-start.9
  19.9 3.7 %all-to-all-start.1 = ((bf16[32,160,128]{2,1,0:T(8,128)(2,1)}), bf16[32,160,128]{2,1,0:T(8,128)(2,1)S(1)}, u32[]{:S(2)}, u32[]{:S(2)}) async-start(bf16[32,160,128]{2,1,0:T(8,128)(2,1)} %shard_map.225), calls=%async_computation.1 | async-start | bytes 2621440 | tf_op jit(solution)/shard_map/all_to_all | solution.py:470
  23.6 0.0 copy-done.10
  23.6 0.0 copy-done.11
  23.6 0.2 reshape.32
  23.8 0.1 copy.25
  24.0 19.0 %collective-permute-done.1.high_ref = bf16[320,512]{1,0:T(8,128)(2,1)S(1)} collective-permute-done((bf16[320,512]{1,0:T(8,128)(2,1)S(1)}, bf16[320,512]{1,0:T(8,128)(2,1)S(1)}, u32[]{:S(2)}, u32[]{:S(2)}) %collective-permute-start.1) | collective-permute-done | bytes 327712 | tf_op jit(solution)/shard_map/ppermute | solution.py:483
  43.0 0.0 collective-permute-done.low_ref
  43.0 0.0 copy-done
  43.0 0.0 copy-done.1
  43.0 0.0 copy-done.2
  43.0 0.0 copy-done.3
  43.0 0.0 copy-done.4
  43.0 0.0 copy-done.5
  43.0 0.0 copy-done.6
  43.0 0.0 copy-done.7
  43.0 0.0 copy-done.8
  43.1 0.0 copy-done.9
  43.1 9.2 %shard_map.226 = (f32[304,512]{1,0:T(8,128)}, f32[272,256]{1,0:T(8,128)}, bf16[2,384,1024]{2,1,0:T(8,128)(2,1)}, s32[2,1,1024]{2,1,0:T(1,128)}) custom-call(bf16[320,512]{1,0:T(8,128)(2,1)S(1)} %get-tuple-element.33.table_ref, bf16[320,512]{1,0:T(8,128)(2,1)S(1)} %collective-permute-done.low_ref, bf16[320,512]{1,0:T(8,128)(2,1)S(1)} %collective-permute-done.1.high_ref, ...), custom_call_target="tpu_custom_call" | custom-call | flops 40000000000 | bytes 8000000 | tf_op jit(solution)/shard_map/pallas_call | solution.py:564
  52.3 4.5 %all-to-all-done.1.reply_ref = bf16[32,160,128]{2,1,0:T(8,128)(2,1)S(1)} async-done(((bf16[32,160,128]{2,1,0:T(8,128)(2,1)}), bf16[32,160,128]{2,1,0:T(8,128)(2,1)S(1)}, u32[]{:S(2)}, u32[]{:S(2)}) %all-to-all-start.1) | async-done | bytes 1310752 | tf_op jit(solution)/shard_map/all_to_all | solution.py:470
  56.8 4.1 %shard_map.227 = (bf16[304,512]{1,0:T(8,128)(2,1)S(1)}, bf16[32,3,4,128]{3,2,1,0:T(4,128)(2,1)S(1)}) custom-call(bf16[32,160,128]{2,1,0:T(8,128)(2,1)S(1)} %all-to-all-done.1.reply_ref, bf16[304,512]{1,0:T(8,128)(2,1)S(1)} %copy-done, s32[2,1,1024]{2,1,0:T(1,128)} %get-tuple-element.36.code_hbm, bf16[2,384,1024]{2,1,0:T(8,128)(2,1)} %get-tuple-element.37.recv_hbm, ...), custom_call_target="tpu_custom_call" | custom-call | tf_op jit(solution)/shard_map/pallas_call | solution.py:606
  60.9 9.7 %all_to_all.21.parts_ref = bf16[32,3,4,128]{3,2,1,0:T(4,128)(2,1)S(1)} all-to-all(bf16[32,3,4,128]{3,2,1,0:T(4,128)(2,1)S(1)} %get-tuple-element.40), channel_id=1, replica_groups=mesh['dom'=4,'sub'=8] {'dom','sub'}, dimensions={0} | all-to-all | bytes 196608 | tf_op jit(solution)/shard_map/all_to_all | solution.py:470
  70.6 0.1 shard_map.228
  70.7 9.3 %all_to_all.22.blocks_ref = bf16[32,3,4,128]{3,2,1,0:T(4,128)(2,1)S(1)} all-to-all(bf16[32,3,4,128]{3,2,1,0:T(4,128)(2,1)S(1)} %shard_map.228), channel_id=1, replica_groups=mesh['dom'=4,'sub'=8] {'dom','sub'}, dimensions={0} | all-to-all | bytes 196608 | tf_op jit(solution)/shard_map/all_to_all | solution.py:470
  80.0 1.1 %shard_map.229 = (bf16[304,512]{1,0:T(8,128)(2,1)}, f32[128,128]{1,0:T(8,128)}, f32[1,128]{1,0:T(1,128)}, f32[1,128]{1,0:T(1,128)}, f32[144,128]{1,0:T(8,128)}, ...) custom-call(bf16[32,3,4,128]{3,2,1,0:T(4,128)(2,1)S(1)} %all_to_all.22.blocks_ref, ...), custom_call_target="tpu_custom_call" | custom-call | tf_op jit(solution)/shard_map/pallas_call | solution.py:632
  (2 shorter events, 0.0 us)
Async XLA Ops:
  15.9 27.1 %collective-permute-start.1 = (bf16[320,512]{1,0:T(8,128)(2,1)S(1)}, bf16[320,512]{1,0:T(8,128)(2,1)S(1)}, u32[]{:S(2)}, u32[]{:S(2)}) collective-permute-start(bf16[320,512]{1,0:T(8,128)(2,1)S(1)} %get-tuple-element.33.table_ref), channel_id=1, source_target_pairs={{0,7},{1,0},{2,1},{3,2},{4,3},{5,4},{6,5},{7,6},{8,15},{9,8},{10,9... | collective-permute-start | bytes 983048 | tf_op jit(solution)/shard_map/ppermute | solution.py:483
  16.5 26.5 %collective-permute-start = (bf16[320,512]{1,0:T(8,128)(2,1)S(1)}, bf16[320,512]{1,0:T(8,128)(2,1)S(1)}, u32[]{:S(2)}, u32[]{:S(2)}) collective-permute-start(bf16[320,512]{1,0:T(8,128)(2,1)S(1)} %get-tuple-element.33.table_ref), channel_id=1, source_target_pairs={{0,1},{1,2},{2,3},{3,4},{4,5},{5,6},{6,7},{7,0},{8,9},{9,10},{10,1... | collective-permute-start | bytes 983048 | tf_op jit(solution)/shard_map/ppermute | solution.py:483
  19.7 3.9 %copy-start.10 = (s32[3072]{0:T(1024)S(1)}, s32[3072]{0:T(1024)}, u32[]{:S(2)}) copy-start(s32[3072]{0:T(1024)} %param.20) | copy-start | bytes 36868
  19.7 3.9 %copy-start.11 = (s32[3072]{0:T(1024)S(1)}, s32[3072]{0:T(1024)}, u32[]{:S(2)}) copy-start(s32[3072]{0:T(1024)} %param.21) | copy-start | bytes 36868
  19.7 23.2 %copy-start = (bf16[304,512]{1,0:T(8,128)(2,1)S(1)}, bf16[304,512]{1,0:T(8,128)(2,1)}, u32[]{:S(2)}) copy-start(bf16[304,512]{1,0:T(8,128)(2,1)} %cot_ref.3) | copy-start | bytes 933892
  19.8 23.2 %copy-start.1 = (bf16[144,128]{1,0:T(8,128)(2,1)S(1)}, bf16[144,128]{1,0:T(8,128)(2,1)}, u32[]{:S(2)}) copy-start(bf16[144,128]{1,0:T(8,128)(2,1)} %w_two_hbm.1) | copy-start | bytes 110596
  19.8 23.2 %copy-start.2 = (bf16[128,128]{1,0:T(8,128)(2,1)S(1)}, bf16[128,128]{1,0:T(8,128)(2,1)}, u32[]{:S(2)}) copy-start(bf16[128,128]{1,0:T(8,128)(2,1)} %w_one_hbm.1) | copy-start | bytes 98308
  19.8 23.2 %copy-start.3 = (bf16[64,64]{1,0:T(8,128)(2,1)S(1)}, bf16[64,64]{1,0:T(8,128)(2,1)}, u32[]{:S(2)}) copy-start(bf16[64,64]{1,0:T(8,128)(2,1)} %w_scal_ref.3) | copy-start | bytes 24580
  19.8 23.2 %copy-start.4 = (bf16[32,32]{1,0:T(8,128)(2,1)S(1)}, bf16[32,32]{1,0:T(8,128)(2,1)}, u32[]{:S(2)}) copy-start(bf16[32,32]{1,0:T(8,128)(2,1)} %w_vec_ref.3) | copy-start | bytes 6148
  19.8 23.2 %copy-start.5 = (bf16[16,16]{1,0:T(8,128)(2,1)S(1)}, bf16[16,16]{1,0:T(8,128)(2,1)}, u32[]{:S(2)}) copy-start(bf16[16,16]{1,0:T(8,128)(2,1)} %w_ten_ref.3) | copy-start | bytes 1540
  19.8 23.2 %copy-start.6 = (f32[128]{0:T(128)S(1)}, f32[128]{0:T(128)}, u32[]{:S(2)}) copy-start(f32[128]{0:T(128)} %param.28) | copy-start | bytes 1540
  19.8 23.2 %copy-start.7 = (f32[128]{0:T(128)S(1)}, f32[128]{0:T(128)}, u32[]{:S(2)}) copy-start(f32[128]{0:T(128)} %param.29) | copy-start | bytes 1540
  19.8 23.2 %copy-start.8 = (s32[2048]{0:T(1024)S(1)}, s32[2048]{0:T(1024)}, u32[]{:S(2)}) copy-start(s32[2048]{0:T(1024)} %param.25) | copy-start | bytes 24580
  19.8 23.2 %copy-start.9 = (s32[2048]{0:T(1024)S(1)}, s32[2048]{0:T(1024)}, u32[]{:S(2)}) copy-start(s32[2048]{0:T(1024)} %param.26) | copy-start | bytes 24580
  19.9 36.9 %all-to-all-start.1 = ((bf16[32,160,128]{2,1,0:T(8,128)(2,1)}), bf16[32,160,128]{2,1,0:T(8,128)(2,1)S(1)}, u32[]{:S(2)}, u32[]{:S(2)}) async-start(bf16[32,160,128]{2,1,0:T(8,128)(2,1)} %shard_map.225), calls=%async_computation.1 | async-start | bytes 2621440 | tf_op jit(solution)/shard_map/all_to_all | solution.py:470
where the time goes:
time: 81.3 us; the launch traced here: 81 us
  blocking collectives  33.2 us (41%)
  waiting for transfers between devices  23.5 us (29%)
  Pallas kernels  17.3 us (21%)
  starting transfers between devices  5.73 us (7%)
  between operations  0.88 us (1%)
    all_to_all x3, blocking collectives, exchange(): return lax.all_to_all(blocks, axes, split_axis=0, concat_axis=0, tiled=True)  33.2 us
    ppermute x2, waiting for transfers between devices, from_behind(): lax.ppermute(shard, axis, [(i, (i + by) % peers) for i in range(peers)])  19 us
    pallas_call x1, Pallas kernels, on_device(): call(mesh_kernel, (pltpu.HBM((FEAT, node_count), f32), pltpu.HBM((mesh_ro...  9.19 us
    all_to_all x1, waiting for transfers between devices, exchange(): return lax.all_to_all(blocks, axes, split_axis=0, concat_axis=0, tiled=True)  4.51 us
    pallas_call x1, Pallas kernels, on_device(): call(functools.partial(contact_kernel, slot, grad_scale), (shaped((FEAT,...  4.1 us
    all_to_all x1, starting transfers between devices, exchange(): return lax.all_to_all(blocks, axes, split_axis=0, concat_axis=0, tiled=True)  3.7 us
    ppermute x2, starting transfers between devices, from_behind(): lax.ppermute(shard, axis, [(i, (i + by) % peers) for i in range(peers)])  2.03 us
    pallas_call x1, Pallas kernels, on_device(): call(functools.partial(contact_gather_kernel, slot), pltpu.HBM((device_co...  1.79 us
  transfers between devices with their start and end apart: 3, of which 2 were waited for; matrix products, arithmetic and copies ran while one was open for 0% of the time, Pallas kernels for 14%

commit v1 on v0

--- a/solution.py
+++ b/solution.py
@@ -17,7 +17,7 @@
 FEAT = CS + 3 * CV + 9 * CT
 ROWS = 320
 LANES = 128
-FINE = 4
+FINE = 2
 CHUNK = 512
 WIDE = 1024
 VMEM_BYTES = 48 * 1024 * 1024
@@ -202,14 +202,16 @@
     agg_out_ref,
     grads_out_ref,
     recv_out_ref,
+    first_out_ref,
     code_out_ref,
+    layers_out_ref,
+    rows_out_ref,
     agg_ref,
     grads_ref,
     recv_ref,
     receive_ref,
     source_ref,
     block_ref,
-    contact_ref,
     sems,
 ):
     node_count = table_ref.shape[1]
@@ -247,16 +249,20 @@
         )
         agg_ref[...] += message
         add_grads(grads_ref, grads)
-    contact_ref[...] = jnp.where(mask_ref[...] != 0, dst_ref[...], -1)
-    for chunk in range(contact_ref.shape[0]):
-        recv_ref[chunk] = dot(
-            receive_ref[...], one_hot(contact_ref[chunk], node_count)
+    code_out_ref[...] = jnp.where(mask_ref[...] != 0, dst_ref[...], -1)
+    for chunk in range(code_out_ref.shape[0]):
+        target = first_out_ref if chunk == 0 else recv_ref.at[chunk - 1]
+        target[...] = dot(
+            receive_ref[...], one_hot(code_out_ref[chunk], node_count)
         ).astype(jnp.bfloat16)
+    layers_out_ref[:HID] = w_one
+    layers_out_ref[HID:] = w_two
+    rows = lax.broadcasted_iota(jnp.int32, (8, HID), 0)
+    rows_out_ref[...] = jnp.where(rows == 0, b_one_ref[...], w_dist_ref[...])
     copies = [
         pltpu.make_async_copy(agg_ref, agg_out_ref, sems.at[0]),
         pltpu.make_async_copy(grads_ref, grads_out_ref, sems.at[1]),
         pltpu.make_async_copy(recv_ref, recv_out_ref, sems.at[2]),
-        pltpu.make_async_copy(contact_ref, code_out_ref, sems.at[3]),
     ]
     for copy in copies:
         copy.start()
@@ -268,39 +274,31 @@
     slot,
     grad_scale,
     reply_ref,
-    cot_ref,
-    code_hbm,
+    first_ref,
+    code_ref,
+    layers_ref,
+    rows_ref,
     recv_hbm,
     mesh_agg_hbm,
     mesh_grads_hbm,
-    w_one_hbm,
-    w_two_hbm,
-    b_one_hbm,
-    w_dist_hbm,
+    cot_hbm,
     agg_out_ref,
     packed_ref,
-    code_ref,
     recv_ref,
     agg_ref,
     grads_ref,
-    w_one_ref,
-    w_two_ref,
-    b_one_ref,
-    w_dist_ref,
+    cot_ref,
     src_scr,
     packed_scr,
     sems,
 ):
     chunks = code_ref.shape[0]
     sources = [
-        (b_one_hbm, b_one_ref),
-        (w_dist_hbm, w_dist_ref),
-        (w_one_hbm, w_one_ref),
-        (w_two_hbm, w_two_ref),
-        (code_hbm, code_ref),
+        (recv_hbm, recv_ref),
+        (mesh_agg_hbm, agg_ref),
+        (mesh_grads_hbm, grads_ref),
+        (cot_hbm, cot_ref),
     ]
-    sources += [(recv_hbm.at[chunk], recv_ref.at[chunk]) for chunk in range(chunks)]
-    sources += [(mesh_agg_hbm, agg_ref), (mesh_grads_hbm, grads_ref)]
     copies = [
         pltpu.make_async_copy(source, target, sems.at[at])
         for at, (source, target) in enumerate(sources)
@@ -321,18 +319,16 @@
             ],
             0,
         )[:ROWS]
-    for copy in copies[:6]:
-        copy.wait()
-    w_one = w_one_ref[...]
-    w_two = w_two_ref[...]
-    b_column, dist_column = as_columns(b_one_ref[...], w_dist_ref[...])
+    w_one = layers_ref[:HID]
+    w_two = layers_ref[HID:]
+    b_column, dist_column = as_columns(rows_ref[0:1], rows_ref[1:2])
     weights = (dist_column, w_two, w_two.T)
     for chunk in range(chunks):
         src_rows = src_scr[chunk]
         if chunk == 1:
-            for copy in copies[6:]:
+            for copy in copies:
                 copy.wait()
-        recv = recv_ref[chunk]
+        recv = first_ref[...] if chunk == 0 else recv_ref[chunk - 1]
         inputs = jnp.concatenate([recv[FEAT + 16 :], src_rows[:CS]], 0)
         message, grads = edge_math(
             src_rows.astype(jnp.float32),
@@ -358,27 +354,31 @@
     cot = cot_ref[...]
     low = HID + GATES
     packed_scr[:low] = grads_ref[:, :LANES] * grad_scale
-    packed_scr[low : low + CS] = jnp.concatenate(
-        [
-            dot(cot[:CS], agg_rows[:CS], 1, 1) * grad_scale,
-            jnp.zeros((CS, LANES - CS), jnp.float32),
-        ],
-        1,
-    )
+    scal = dot(cot[:CS], agg_rows[:CS], 1, 1) * grad_scale
+    packed_scr[low : low + CS // 2] = jnp.concatenate([scal[: CS // 2], scal[CS // 2 :]], 1)
+    low = low + CS // 2
     mixed = dot(cot[CS:], agg_rows[CS:], 1, 1)
     grad_vec = jnp.zeros((CV, CV), jnp.float32)
     for k in range(3):
         rows = slice(k * CV, (k + 1) * CV)
         grad_vec = grad_vec + mixed[rows, rows]
-    packed_scr[low : low + CV, CS : CS + CV] = grad_vec * grad_scale
+    each = CV * CV // LANES
+    packed_scr[low : low + each] = grad_scale * jnp.concatenate(
+        [grad_vec[at : at + each] for at in range(0, CV, each)], 1
+    )
+    low = low + each
     grad_ten = jnp.zeros((CT, CT), jnp.float32)
     for m in range(9):
         rows = slice(3 * CV + m * CT, 3 * CV + (m + 1) * CT)
         grad_ten = grad_ten + mixed[rows, rows]
-    packed_scr[low : low + CT, CS + CV : CS + CV + CT] = grad_ten * grad_scale
-    extra = (grads_ref[:HID, LANES:] * grad_scale).T[:16]
-    rows = lax.broadcasted_iota(jnp.int32, (16, LANES), 0)
-    packed_scr[low + CS :] = jnp.where(rows == 1, extra[1:2] + extra[2:3], extra)
+    each = CT * CT // LANES
+    packed_scr[low : low + each] = grad_scale * jnp.concatenate(
+        [grad_ten[at : at + each] for at in range(0, CT, each)], 1
+    )
+    low = low + each
+    extra = (grads_ref[:HID, LANES:] * grad_scale).T
+    packed_scr[low : low + 1] = extra[0:1]
+    packed_scr[low + 1 : low + 2] = extra[1:2] + extra[2:3]
     packed = packed_scr[...].astype(jnp.bfloat16)
     tiles = packed_ref.shape[1]
     for peer in range(packed_ref.shape[0]):
@@ -432,14 +432,20 @@
     for at in range(0, GATES, FINE):
         two_ref[at : at + FINE] = rows_of(HID + at)
     low = HID + GATES
-    for at in range(0, CS, FINE):
+    for at in range(0, CS // 2, FINE):
         rows = rows_of(low + at)
         scal_ref[at : at + FINE] = rows[:, :CS]
-        if at < CV:
-            vec_ref[at : at + FINE] = rows[:, CS : CS + CV]
-        if at < CT:
-            ten_ref[at : at + FINE] = rows[:, CS + CV : CS + CV + CT]
-    extra = rows_of(low + CS)
+        scal_ref[CS // 2 + at : CS // 2 + at + FINE] = rows[:, CS:]
+    low = low + CS // 2
+    for ref, width in ((vec_ref, CV), (ten_ref, CT)):
+        each = width * width // LANES
+        for at in range(0, each, FINE):
+            rows = rows_of(low + at)
+            for piece in range(width // each):
+                to = piece * each + at
+                ref[to : to + FINE] = rows[:, piece * width : (piece + 1) * width]
+        low = low + each
+    extra = rows_of(low)
     bias_ref[...] = extra[0:1]
     dist_ref[...] = extra[1:2]
 
@@ -561,26 +567,28 @@
     contact_mask = contact_mask.reshape(wides, 1, WIDE)
     mesh_rows = HID + GATES
     recv_rows = FEAT + 16 + CS
-    mesh_agg, mesh_grads, recv, contact_code = call(
+    mesh_agg, mesh_grads, recv, first, contact_code, layers, rows = call(
         mesh_kernel,
         (
             pltpu.HBM((FEAT, node_count), f32),
             pltpu.HBM((mesh_rows, 2 * LANES), f32),
-            pltpu.HBM((wides, recv_rows, WIDE), bf16),
-            pltpu.HBM((wides, 1, WIDE), jnp.int32),
+            pltpu.HBM((wides - 1, recv_rows, WIDE), bf16),
+            shaped((recv_rows, WIDE), bf16),
+            shaped((wides, 1, WIDE), jnp.int32),
+            shaped((mesh_rows, HID), bf16),
+            shaped((8, HID), f32),
         ),
         (
             pltpu.VMEM((FEAT, node_count), f32),
             pltpu.VMEM((mesh_rows, 2 * LANES), f32),
-            pltpu.VMEM((wides, recv_rows, WIDE), bf16),
+            pltpu.VMEM((wides - 1, recv_rows, WIDE), bf16),
             pltpu.VMEM((recv_rows, node_count), bf16),
             pltpu.VMEM((ROWS, 3 * node_count), bf16),
             pltpu.VMEM((FEAT, FEAT), bf16),
-            pltpu.VMEM((wides, 1, WIDE), jnp.int32),
-            pltpu.SemaphoreType.DMA((4,)),
+            pltpu.SemaphoreType.DMA((3,)),
         ),
         in_specs=[IN_VMEM] * 14,
-        out_specs=(IN_HBM,) * 4,
+        out_specs=(IN_HBM,) * 3 + (IN_VMEM,) * 4,
         cost_estimate=pl.CostEstimate(
             flops=40_000_000_000, bytes_accessed=8_000_000, transcendentals=400_000
         ),
@@ -600,33 +608,30 @@
         contact_dst,
         contact_mask,
     )
-    packed_rows = mesh_rows + CS + 16
+    packed_rows = mesh_rows + (CS * CS + CV * CV + CT * CT) // LANES + 2
     tiles = -(-packed_rows // (FINE * device_count))
     share = (device_count, tiles, FINE, LANES)
     agg_rows, packed = call(
         functools.partial(contact_kernel, slot, grad_scale),
         (shaped((FEAT, node_count), bf16), shaped(share, bf16)),
         (
-            pltpu.VMEM((wides, 1, WIDE), jnp.int32),
-            pltpu.VMEM((wides, recv_rows, WIDE), bf16),
+            pltpu.VMEM((wides - 1, recv_rows, WIDE), bf16),
             pltpu.VMEM((FEAT, node_count), f32),
             pltpu.VMEM((mesh_rows, 2 * LANES), f32),
-            pltpu.VMEM((HID, 2 * CS), bf16),
-            pltpu.VMEM((GATES, HID), bf16),
-            pltpu.VMEM((1, HID), f32),
-            pltpu.VMEM((1, HID), f32),
+            pltpu.VMEM((FEAT, node_count), bf16),
             pltpu.VMEM((wides, ROWS, WIDE), bf16),
             pltpu.VMEM((packed_rows, LANES), f32),
-            pltpu.SemaphoreType.DMA((wides + 7,)),
-        ),
-        in_specs=[IN_VMEM] * 2 + [IN_HBM] * 8,
+            pltpu.SemaphoreType.DMA((4,)),
+        ),
+        in_specs=[IN_VMEM] * 5 + [IN_HBM] * 4,
         out_specs=(IN_VMEM, IN_VMEM),
     )(
         replies,
-        node_cot,
-        *in_hbm(
-            contact_code, recv, mesh_agg, mesh_grads, w_one, w_two, b_one[None], w_dist[None]
-        ),
+        first,
+        contact_code,
+        layers,
+        rows,
+        *in_hbm(recv, mesh_agg, mesh_grads, node_cot),
     )
     shares = call(sum_kernel, shaped(share, bf16))(exchange(packed))
     node_out, one, bias, dist, two, scal, vec, ten = call(

time: 81.3 us -> 80.5 us (level)
  local copies, waits for them, and re-layouts: 0.41 us -> 2.45 us
  waiting for transfers between devices: 23.5 us -> 21.7 us
  Pallas kernels: 17.3 us -> 16.4 us
    unnamed x24, local copies, waits for them, and re-layouts: 0.08 us -> 2.12 us
    all_to_all x1, waiting for transfers between devices: 4.51 us -> 2.66 us  [exchange(): return lax.all_to_all(blocks, axes, split_axis=0, concat_axis=0, tiled=True)]
  transfers between devices with their start and end apart: 3 -> 3, of which waited for: 2 -> 2; matrix products, arithmetic and copies ran while one was open for 0% -> 0% of each run, Pallas kernels for 14% -> 13%
where the time goes in v1:
time: 80.5 us; the launch traced here: 80.2 us
  blocking collectives  33 us (41%)
  waiting for transfers between devices  21.7 us (27%)
  Pallas kernels  16.4 us (20%)
  starting transfers between devices  5.73 us (7%)
  local copies, waits for them, and re-layouts  2.45 us (3%)
  between operations  0.85 us (1%)
    all_to_all x3, blocking collectives, exchange(): return lax.all_to_all(blocks, axes, split_axis=0, concat_axis=0, tiled=True)  33 us
    ppermute x2, waiting for transfers between devices, from_behind(): lax.ppermute(shard, axis, [(i, (i + by) % peers) for i in range(peers)])  19.1 us
    pallas_call x1, Pallas kernels, on_device(): call(mesh_kernel, (pltpu.HBM((FEAT, node_count), f32), pltpu.HBM((mesh_ro...  8.95 us
    all_to_all x1, starting transfers between devices, exchange(): return lax.all_to_all(blocks, axes, split_axis=0, concat_axis=0, tiled=True)  3.7 us
    pallas_call x1, Pallas kernels, on_device(): call(functools.partial(contact_kernel, slot, grad_scale), (shaped((FEAT,...  3.5 us
    all_to_all x1, waiting for transfers between devices, exchange(): return lax.all_to_all(blocks, axes, split_axis=0, concat_axis=0, tiled=True)  2.66 us
    unnamed x24, local copies, waits for them, and re-layouts  2.12 us
    ppermute x2, starting transfers between devices, from_behind(): lax.ppermute(shard, axis, [(i, (i + by) % peers) for i in range(peers)])  2.03 us
  transfers between devices with their start and end apart: 3, of which 2 were waited for; matrix products, arithmetic and copies ran while one was open for 0% of the time, Pallas kernels for 13%

profile of v1, /device:TPU:0, one launch (start us, length us, event | category | flops | bytes accessed | tf_op | source)
XLA Modules:
  0.0 80.2 jit_solution(2858358297131332446)
XLA Ops:
  0.6 1.0 %shard_map.224 = (bf16[320,512]{1,0:T(8,128)(2,1)S(1)}, s32[32,1,64]{2,1,0:T(1,128)S(1)}) custom-call(bf16[304,512]{1,0:T(8,128)(2,1)} %feat_ref.1, bf16[3,512]{1,0:T(4,128)(2,1)} %pos_ref.1, s32[1,512]{1,0:T(1,128)} %bitcast.16, s32[1,512]{1,0:T(1,128)} %bitcast.17, s32[16,128]{1,0:T(8,128)} %bitcast.15), custom_call_target="tpu_custom_call" | custom-call | tf_op jit(solution)/shard_map/pallas_call | solution.py:521
  1.7 14.2 %all_to_all.20.wanted_ref = s32[32,1,64]{2,1,0:T(1,128)S(1)} all-to-all(s32[32,1,64]{2,1,0:T(1,128)S(1)} %get-tuple-element.33), channel_id=1, replica_groups=mesh['dom'=4,'sub'=8] {'dom','sub'}, dimensions={0} | all-to-all | bytes 16384 | tf_op jit(solution)/shard_map/all_to_all | solution.py:476
  15.9 0.6 collective-permute-start.1
  16.5 1.4 %collective-permute-start = (bf16[320,512]{1,0:T(8,128)(2,1)S(1)}, bf16[320,512]{1,0:T(8,128)(2,1)S(1)}, u32[]{:S(2)}, u32[]{:S(2)}) collective-permute-start(bf16[320,512]{1,0:T(8,128)(2,1)S(1)} %get-tuple-element.36.table_ref), channel_id=1, source_target_pairs={{0,1},{1,2},{2,3},{3,4},{4,5},{5,6},{6,7},{7,0},{8,9},{9,10},{10,1... | collective-permute-start | bytes 983048 | tf_op jit(solution)/shard_map/ppermute | solution.py:489
  17.9 1.8 %shard_map.225 = bf16[32,160,128]{2,1,0:T(8,128)(2,1)} custom-call(bf16[320,512]{1,0:T(8,128)(2,1)S(1)} %get-tuple-element.36.table_ref, s32[32,1,64]{2,1,0:T(1,128)S(1)} %all_to_all.20.wanted_ref), custom_call_target="tpu_custom_call" | custom-call | tf_op jit(solution)/shard_map/pallas_call | solution.py:549
  19.7 0.0 copy-start.10
  19.7 0.0 copy-start.11
  19.7 0.0 copy-start
  19.7 0.0 copy-start.1
  19.8 0.0 copy-start.2
  19.8 0.0 copy-start.3
  19.8 0.0 copy-start.4
  19.8 0.0 copy-start.6
  19.8 0.0 copy-start.7
  19.8 3.7 %all-to-all-start.1 = ((bf16[32,160,128]{2,1,0:T(8,128)(2,1)}), bf16[32,160,128]{2,1,0:T(8,128)(2,1)S(1)}, u32[]{:S(2)}, u32[]{:S(2)}) async-start(bf16[32,160,128]{2,1,0:T(8,128)(2,1)} %shard_map.225), calls=%async_computation.1 | async-start | bytes 2621440 | tf_op jit(solution)/shard_map/all_to_all | solution.py:476
  23.5 0.0 copy-done.10
  23.5 0.0 copy-done.11
  23.6 0.2 reshape.32
  23.8 0.1 copy.25
  23.9 19.1 %collective-permute-done.1.high_ref = bf16[320,512]{1,0:T(8,128)(2,1)S(1)} collective-permute-done((bf16[320,512]{1,0:T(8,128)(2,1)S(1)}, bf16[320,512]{1,0:T(8,128)(2,1)S(1)}, u32[]{:S(2)}, u32[]{:S(2)}) %collective-permute-start.1) | collective-permute-done | bytes 327712 | tf_op jit(solution)/shard_map/ppermute | solution.py:489
  43.0 0.0 collective-permute-done.low_ref
  43.0 0.0 copy-done
  43.0 0.0 copy-done.1
  43.0 0.0 copy-done.2
  43.0 0.0 copy-done.3
  43.0 0.0 copy-done.4
  43.0 0.0 copy-done.6
  43.0 0.0 copy-done.7
  43.0 0.0 copy-start.5
  43.1 0.7 copy-done.5
  43.8 0.0 copy-start.8
  43.8 0.7 copy-done.8
  44.5 0.0 copy-start.9
  44.5 0.7 copy-done.9
  45.1 9.0 %shard_map.226 = (f32[304,512]{1,0:T(8,128)}, f32[272,256]{1,0:T(8,128)}, bf16[1,384,1024]{2,1,0:T(8,128)(2,1)}, bf16[384,1024]{1,0:T(8,128)(2,1)S(1)}, s32[2,1,...) custom-call(bf16[320,512]{1,0:T(8,128)(2,1)S(1)} %get-tuple-element.36.table_ref, ...), custom_call_target="tpu_custom_call" | custom-call | flops 40000000000 | bytes 8000000 | tf_op jit(solution)/shard_map/pallas_call | solution.py:570
  54.1 2.7 %all-to-all-done.1.reply_ref = bf16[32,160,128]{2,1,0:T(8,128)(2,1)S(1)} async-done(((bf16[32,160,128]{2,1,0:T(8,128)(2,1)}), bf16[32,160,128]{2,1,0:T(8,128)(2,1)S(1)}, u32[]{:S(2)}, u32[]{:S(2)}) %all-to-all-start.1) | async-done | bytes 1310752 | tf_op jit(solution)/shard_map/all_to_all | solution.py:476
  56.7 3.5 %shard_map.227 = (bf16[304,512]{1,0:T(8,128)(2,1)S(1)}, bf16[32,5,2,128]{3,2,1,0:T(2,128)(2,1)S(1)}) custom-call(bf16[32,160,128]{2,1,0:T(8,128)(2,1)S(1)} %all-to-all-done.1.reply_ref, bf16[384,1024]{1,0:T(8,128)(2,1)S(1)} %get-tuple-element.39.first_ref, s32[2,1,1024]{2,1,0:T(1,128)S(1)} %get-tuple-element.40.code_ref, ...), custom_call_target="tpu_custom_call" | custom-call | tf_op jit(solution)/shard_map/pallas_call | solution.py:614
  60.2 9.6 %all_to_all.21.parts_ref = bf16[32,5,2,128]{3,2,1,0:T(2,128)(2,1)S(1)} all-to-all(bf16[32,5,2,128]{3,2,1,0:T(2,128)(2,1)S(1)} %get-tuple-element.46), channel_id=1, replica_groups=mesh['dom'=4,'sub'=8] {'dom','sub'}, dimensions={0} | all-to-all | bytes 163840 | tf_op jit(solution)/shard_map/all_to_all | solution.py:476
  69.8 0.1 shard_map.228
  69.9 9.1 %all_to_all.22.blocks_ref = bf16[32,5,2,128]{3,2,1,0:T(2,128)(2,1)S(1)} all-to-all(bf16[32,5,2,128]{3,2,1,0:T(2,128)(2,1)S(1)} %shard_map.228), channel_id=1, replica_groups=mesh['dom'=4,'sub'=8] {'dom','sub'}, dimensions={0} | all-to-all | bytes 163840 | tf_op jit(solution)/shard_map/all_to_all | solution.py:476
  79.1 1.1 %shard_map.229 = (bf16[304,512]{1,0:T(8,128)(2,1)}, f32[128,128]{1,0:T(8,128)}, f32[1,128]{1,0:T(1,128)}, f32[1,128]{1,0:T(1,128)}, f32[144,128]{1,0:T(8,128)}, ...) custom-call(bf16[32,5,2,128]{3,2,1,0:T(2,128)(2,1)S(1)} %all_to_all.22.blocks_ref, ...), custom_call_target="tpu_custom_call" | custom-call | tf_op jit(solution)/shard_map/pallas_call | solution.py:637
  (2 shorter events, 0.0 us)
Async XLA Ops:
  15.9 27.1 %collective-permute-start.1 = (bf16[320,512]{1,0:T(8,128)(2,1)S(1)}, bf16[320,512]{1,0:T(8,128)(2,1)S(1)}, u32[]{:S(2)}, u32[]{:S(2)}) collective-permute-start(bf16[320,512]{1,0:T(8,128)(2,1)S(1)} %get-tuple-element.36.table_ref), channel_id=1, source_target_pairs={{0,7},{1,0},{2,1},{3,2},{4,3},{5,4},{6,5},{7,6},{8,15},{9,8},{10,9... | collective-permute-start | bytes 983048 | tf_op jit(solution)/shard_map/ppermute | solution.py:489
  16.5 26.5 %collective-permute-start = (bf16[320,512]{1,0:T(8,128)(2,1)S(1)}, bf16[320,512]{1,0:T(8,128)(2,1)S(1)}, u32[]{:S(2)}, u32[]{:S(2)}) collective-permute-start(bf16[320,512]{1,0:T(8,128)(2,1)S(1)} %get-tuple-element.36.table_ref), channel_id=1, source_target_pairs={{0,1},{1,2},{2,3},{3,4},{4,5},{5,6},{6,7},{7,0},{8,9},{9,10},{10,1... | collective-permute-start | bytes 983048 | tf_op jit(solution)/shard_map/ppermute | solution.py:489
  19.7 3.8 %copy-start.10 = (s32[3072]{0:T(1024)S(1)}, s32[3072]{0:T(1024)}, u32[]{:S(2)}) copy-start(s32[3072]{0:T(1024)} %param.20) | copy-start | bytes 36868
  19.7 3.8 %copy-start.11 = (s32[3072]{0:T(1024)S(1)}, s32[3072]{0:T(1024)}, u32[]{:S(2)}) copy-start(s32[3072]{0:T(1024)} %param.21) | copy-start | bytes 36868
  19.7 23.3 %copy-start = (bf16[304,512]{1,0:T(8,128)(2,1)S(1)}, bf16[304,512]{1,0:T(8,128)(2,1)}, u32[]{:S(2)}) copy-start(bf16[304,512]{1,0:T(8,128)(2,1)} %cot_hbm.1) | copy-start | bytes 933892
  19.7 23.2 %copy-start.1 = (bf16[64,64]{1,0:T(8,128)(2,1)S(1)}, bf16[64,64]{1,0:T(8,128)(2,1)}, u32[]{:S(2)}) copy-start(bf16[64,64]{1,0:T(8,128)(2,1)} %w_scal_ref.3) | copy-start | bytes 24580
  19.8 23.2 %copy-start.2 = (bf16[32,32]{1,0:T(8,128)(2,1)S(1)}, bf16[32,32]{1,0:T(8,128)(2,1)}, u32[]{:S(2)}) copy-start(bf16[32,32]{1,0:T(8,128)(2,1)} %w_vec_ref.3) | copy-start | bytes 6148
  19.8 23.2 %copy-start.3 = (bf16[16,16]{1,0:T(8,128)(2,1)S(1)}, bf16[16,16]{1,0:T(8,128)(2,1)}, u32[]{:S(2)}) copy-start(bf16[16,16]{1,0:T(8,128)(2,1)} %w_ten_ref.3) | copy-start | bytes 1540
  19.8 23.2 %copy-start.4 = (bf16[144,128]{1,0:T(8,128)(2,1)S(1)}, bf16[144,128]{1,0:T(8,128)(2,1)}, u32[]{:S(2)}) copy-start(bf16[144,128]{1,0:T(8,128)(2,1)} %w_two_ref.1) | copy-start | bytes 110596
  19.8 23.2 %copy-start.6 = (s32[2048]{0:T(1024)S(1)}, s32[2048]{0:T(1024)}, u32[]{:S(2)}) copy-start(s32[2048]{0:T(1024)} %param.25) | copy-start | bytes 24580
  19.8 23.2 %copy-start.7 = (s32[2048]{0:T(1024)S(1)}, s32[2048]{0:T(1024)}, u32[]{:S(2)}) copy-start(s32[2048]{0:T(1024)} %param.26) | copy-start | bytes 24580
  19.8 36.9 %all-to-all-start.1 = ((bf16[32,160,128]{2,1,0:T(8,128)(2,1)}), bf16[32,160,128]{2,1,0:T(8,128)(2,1)S(1)}, u32[]{:S(2)}, u32[]{:S(2)}) async-start(bf16[32,160,128]{2,1,0:T(8,128)(2,1)} %shard_map.225), calls=%async_computation.1 | async-start | bytes 2621440 | tf_op jit(solution)/shard_map/all_to_all | solution.py:476
  43.0 0.8 copy-start.5
  43.8 0.7 copy-start.8
  44.5 0.7 copy-start.9

commit v2 on v1

--- a/solution.py
+++ b/solution.py
@@ -406,7 +406,7 @@
     w_scal_ref,
     w_vec_ref,
     w_ten_ref,
-    out_ref,
+    out_hbm,
     one_ref,
     bias_ref,
     dist_ref,
@@ -414,12 +414,16 @@
     scal_ref,
     vec_ref,
     ten_ref,
+    out_ref,
     block_ref,
+    sem,
 ):
     block_diagonal(block_ref, w_scal_ref, w_vec_ref, w_ten_ref)
     out_ref[...] = (
         table_ref[:FEAT].astype(jnp.float32) + dot(block_ref[...], agg_ref[...])
     ).astype(jnp.bfloat16)
+    copy = pltpu.make_async_copy(out_ref, out_hbm, sem)
+    copy.start()
 
     tiles = blocks_ref.shape[1]
 
@@ -448,6 +452,7 @@
     extra = rows_of(low)
     bias_ref[...] = extra[0:1]
     dist_ref[...] = extra[1:2]
+    copy.wait()
 
 
 def call(kernel, out_shape, scratch=(), in_specs=None, out_specs=None, cost_estimate=None):
@@ -543,9 +548,6 @@
         )
     )
     wanted = exchange(requests)
-    wanted, table_late = lax.optimization_barrier((wanted, table))
-    low = from_behind(table_late, "sub", 1)
-    high = from_behind(table_late, "sub", -1)
     found = call(
         functools.partial(contact_gather_kernel, slot),
         pltpu.HBM((device_count, height, LANES), bf16),
@@ -556,7 +558,11 @@
         in_specs=[IN_VMEM, IN_VMEM],
         out_specs=IN_HBM,
     )(table, wanted)
-    found, mesh_senders, edge_mask = lax.optimization_barrier((found, mesh_senders, edge_mask))
+    found, table_late, mesh_senders, edge_mask = lax.optimization_barrier(
+        (found, table, mesh_senders, edge_mask)
+    )
+    low = from_behind(table_late, "sub", 1)
+    high = from_behind(table_late, "sub", -1)
     replies = exchange(found)
     mesh_code = (
         jnp.where(edge_mask != 0, mesh_senders, -1)
@@ -637,7 +643,7 @@
     node_out, one, bias, dist, two, scal, vec, ten = call(
         finish_kernel,
         (
-            shaped((FEAT, node_count), bf16),
+            pltpu.HBM((FEAT, node_count), bf16),
             shaped((HID, 2 * CS), f32),
             shaped((1, HID), f32),
             shaped((1, HID), f32),
@@ -646,7 +652,13 @@
             shaped((CV, CV), f32),
             shaped((CT, CT), f32),
         ),
-        (pltpu.VMEM((FEAT, FEAT), bf16),),
+        (
+            pltpu.VMEM((FEAT, node_count), bf16),
+            pltpu.VMEM((FEAT, FEAT), bf16),
+            pltpu.SemaphoreType.DMA(()),
+        ),
+        in_specs=[IN_VMEM] * 6,
+        out_specs=(IN_HBM,) + (IN_VMEM,) * 7,
     )(exchange(shares), table, agg_rows, w_scal, w_vec, w_ten)
     return node_out, one, bias[0], dist[0], two, scal, vec, ten
 

time: 80.5 us -> 82.3 us (1.022)
  waiting for transfers between devices: 21.7 us -> 23.3 us
    ppermute x2, waiting for transfers between devices: 19.1 us -> 20.3 us  [from_behind(): lax.ppermute(shard, axis, [(i, (i + by) % peers) for i in range(peers)])]
  transfers between devices with their start and end apart: 3 -> 3, of which waited for: 2 -> 2; matrix products, arithmetic and copies ran while one was open for 0% -> 0% of each run, Pallas kernels for 13% -> 11%
where the time goes in v2:
time: 82.3 us; the launch traced here: 82 us
  blocking collectives  32.5 us (39%)
  waiting for transfers between devices  23.3 us (28%)
  Pallas kernels  17.1 us (21%)
  starting transfers between devices  5.77 us (7%)
  local copies, waits for them, and re-layouts  2.45 us (3%)
  between operations  0.85 us (1%)
    all_to_all x3, blocking collectives, exchange(): return lax.all_to_all(blocks, axes, split_axis=0, concat_axis=0, tiled=True)  32.5 us
    ppermute x2, waiting for transfers between devices, from_behind(): lax.ppermute(shard, axis, [(i, (i + by) % peers) for i in range(peers)])  20.3 us
    pallas_call x1, Pallas kernels, on_device(): call(mesh_kernel, (pltpu.HBM((FEAT, node_count), f32), pltpu.HBM((mesh_ro...  8.95 us
    all_to_all x1, starting transfers between devices, exchange(): return lax.all_to_all(blocks, axes, split_axis=0, concat_axis=0, tiled=True)  3.69 us
    pallas_call x1, Pallas kernels, on_device(): call(functools.partial(contact_kernel, slot, grad_scale), (shaped((FEAT,...  3.5 us
    all_to_all x1, waiting for transfers between devices, exchange(): return lax.all_to_all(blocks, axes, split_axis=0, concat_axis=0, tiled=True)  2.97 us
    unnamed x24, local copies, waits for them, and re-layouts  2.12 us
    ppermute x2, starting transfers between devices, from_behind(): lax.ppermute(shard, axis, [(i, (i + by) % peers) for i in range(peers)])  2.08 us
  transfers between devices with their start and end apart: 3, of which 2 were waited for; matrix products, arithmetic and copies ran while one was open for 0% of the time, Pallas kernels for 11%

profile of v2, /device:TPU:0, one launch (start us, length us, event | category | flops | bytes accessed | tf_op | source)
XLA Modules:
  0.0 82.0 jit_solution(7885553684314744741)
XLA Ops:
  0.6 1.0 %shard_map.224 = (bf16[320,512]{1,0:T(8,128)(2,1)S(1)}, s32[32,1,64]{2,1,0:T(1,128)S(1)}) custom-call(bf16[304,512]{1,0:T(8,128)(2,1)} %feat_ref.1, bf16[3,512]{1,0:T(4,128)(2,1)} %pos_ref.1, s32[1,512]{1,0:T(1,128)} %bitcast.16, s32[1,512]{1,0:T(1,128)} %bitcast.17, s32[16,128]{1,0:T(8,128)} %bitcast.15), custom_call_target="tpu_custom_call" | custom-call | tf_op jit(solution)/shard_map/pallas_call | solution.py:526
  1.7 14.2 %all_to_all.20.wanted_ref = s32[32,1,64]{2,1,0:T(1,128)S(1)} all-to-all(s32[32,1,64]{2,1,0:T(1,128)S(1)} %get-tuple-element.32), channel_id=1, replica_groups=mesh['dom'=4,'sub'=8] {'dom','sub'}, dimensions={0} | all-to-all | bytes 16384 | tf_op jit(solution)/shard_map/all_to_all | solution.py:481
  15.9 1.8 %shard_map.225 = bf16[32,160,128]{2,1,0:T(8,128)(2,1)} custom-call(bf16[320,512]{1,0:T(8,128)(2,1)S(1)} %get-tuple-element.34.table_ref, s32[32,1,64]{2,1,0:T(1,128)S(1)} %all_to_all.20.wanted_ref), custom_call_target="tpu_custom_call" | custom-call | tf_op jit(solution)/shard_map/pallas_call | solution.py:551
  17.7 0.0 copy-start.10
  17.7 0.0 copy-start.11
  17.7 0.0 copy-start
  17.7 0.0 copy-start.1
  17.7 0.0 copy-start.2
  17.7 0.0 copy-start.3
  17.8 0.0 copy-start.4
  17.8 0.0 copy-start.6
  17.8 0.0 copy-start.7
  17.8 0.7 collective-permute-start.1
  18.5 1.4 %collective-permute-start = (bf16[320,512]{1,0:T(8,128)(2,1)S(1)}, bf16[320,512]{1,0:T(8,128)(2,1)S(1)}, u32[]{:S(2)}, u32[]{:S(2)}) collective-permute-start(bf16[320,512]{1,0:T(8,128)(2,1)S(1)} %get-tuple-element.34.table_ref), channel_id=1, source_target_pairs={{0,1},{1,2},{2,3},{3,4},{4,5},{5,6},{6,7},{7,0},{8,9},{9,10},{10,1... | collective-permute-start | bytes 983048 | tf_op jit(solution)/shard_map/ppermute | solution.py:494
  19.9 3.7 %all-to-all-start.1 = ((bf16[32,160,128]{2,1,0:T(8,128)(2,1)}), bf16[32,160,128]{2,1,0:T(8,128)(2,1)S(1)}, u32[]{:S(2)}, u32[]{:S(2)}) async-start(bf16[32,160,128]{2,1,0:T(8,128)(2,1)} %shard_map.225), calls=%async_computation.1 | async-start | bytes 2621440 | tf_op jit(solution)/shard_map/all_to_all | solution.py:481
  23.6 0.0 copy-done.10
  23.6 0.0 copy-done.11
  23.6 0.2 reshape.32
  23.8 0.1 copy.25
  24.0 20.3 %collective-permute-done.1.high_ref = bf16[320,512]{1,0:T(8,128)(2,1)S(1)} collective-permute-done((bf16[320,512]{1,0:T(8,128)(2,1)S(1)}, bf16[320,512]{1,0:T(8,128)(2,1)S(1)}, u32[]{:S(2)}, u32[]{:S(2)}) %collective-permute-start.1) | collective-permute-done | bytes 327712 | tf_op jit(solution)/shard_map/ppermute | solution.py:494
  44.3 0.0 collective-permute-done.low_ref
  44.3 0.0 copy-done
  44.3 0.0 copy-done.1
  44.3 0.0 copy-done.2
  44.3 0.0 copy-done.3
  44.3 0.0 copy-done.4
  44.3 0.0 copy-done.6
  44.3 0.0 copy-done.7
  44.3 0.0 copy-start.5
  44.3 0.7 copy-done.5
  45.1 0.0 copy-start.8
  45.1 0.7 copy-done.8
  45.7 0.0 copy-start.9
  45.7 0.7 copy-done.9
  46.4 9.0 %shard_map.226 = (f32[304,512]{1,0:T(8,128)}, f32[272,256]{1,0:T(8,128)}, bf16[1,384,1024]{2,1,0:T(8,128)(2,1)}, bf16[384,1024]{1,0:T(8,128)(2,1)S(1)}, s32[2,1,...) custom-call(bf16[320,512]{1,0:T(8,128)(2,1)S(1)} %get-tuple-element.34.table_ref, ...), custom_call_target="tpu_custom_call" | custom-call | flops 40000000000 | bytes 8000000 | tf_op jit(solution)/shard_map/pallas_call | solution.py:576
  55.4 3.0 %all-to-all-done.1.reply_ref = bf16[32,160,128]{2,1,0:T(8,128)(2,1)S(1)} async-done(((bf16[32,160,128]{2,1,0:T(8,128)(2,1)}), bf16[32,160,128]{2,1,0:T(8,128)(2,1)S(1)}, u32[]{:S(2)}, u32[]{:S(2)}) %all-to-all-start.1) | async-done | bytes 1310752 | tf_op jit(solution)/shard_map/all_to_all | solution.py:481
  58.3 3.5 %shard_map.227 = (bf16[304,512]{1,0:T(8,128)(2,1)S(1)}, bf16[32,5,2,128]{3,2,1,0:T(2,128)(2,1)S(1)}) custom-call(bf16[32,160,128]{2,1,0:T(8,128)(2,1)S(1)} %all-to-all-done.1.reply_ref, bf16[384,1024]{1,0:T(8,128)(2,1)S(1)} %get-tuple-element.37.first_ref, s32[2,1,1024]{2,1,0:T(1,128)S(1)} %get-tuple-element.38.code_ref, ...), custom_call_target="tpu_custom_call" | custom-call | tf_op jit(solution)/shard_map/pallas_call | solution.py:620
  61.8 9.1 %all_to_all.21.parts_ref = bf16[32,5,2,128]{3,2,1,0:T(2,128)(2,1)S(1)} all-to-all(bf16[32,5,2,128]{3,2,1,0:T(2,128)(2,1)S(1)} %get-tuple-element.44), channel_id=1, replica_groups=mesh['dom'=4,'sub'=8] {'dom','sub'}, dimensions={0} | all-to-all | bytes 163840 | tf_op jit(solution)/shard_map/all_to_all | solution.py:481
  71.0 0.1 shard_map.228
  71.1 9.1 %all_to_all.22.blocks_ref = bf16[32,5,2,128]{3,2,1,0:T(2,128)(2,1)S(1)} all-to-all(bf16[32,5,2,128]{3,2,1,0:T(2,128)(2,1)S(1)} %shard_map.228), channel_id=1, replica_groups=mesh['dom'=4,'sub'=8] {'dom','sub'}, dimensions={0} | all-to-all | bytes 163840 | tf_op jit(solution)/shard_map/all_to_all | solution.py:481
  80.2 1.8 %shard_map.229 = (bf16[304,512]{1,0:T(8,128)(2,1)}, f32[128,128]{1,0:T(8,128)}, f32[1,128]{1,0:T(1,128)}, f32[1,128]{1,0:T(1,128)}, f32[144,128]{1,0:T(8,128)}, ...) custom-call(bf16[32,5,2,128]{3,2,1,0:T(2,128)(2,1)S(1)} %all_to_all.22.blocks_ref, ...), custom_call_target="tpu_custom_call" | custom-call | tf_op jit(solution)/shard_map/pallas_call | solution.py:643
  (2 shorter events, 0.0 us)
Async XLA Ops:
  17.7 5.9 %copy-start.10 = (s32[3072]{0:T(1024)S(1)}, s32[3072]{0:T(1024)}, u32[]{:S(2)}) copy-start(s32[3072]{0:T(1024)} %param.20) | copy-start | bytes 36868
  17.7 5.9 %copy-start.11 = (s32[3072]{0:T(1024)S(1)}, s32[3072]{0:T(1024)}, u32[]{:S(2)}) copy-start(s32[3072]{0:T(1024)} %param.21) | copy-start | bytes 36868
  17.7 26.6 %copy-start = (bf16[304,512]{1,0:T(8,128)(2,1)S(1)}, bf16[304,512]{1,0:T(8,128)(2,1)}, u32[]{:S(2)}) copy-start(bf16[304,512]{1,0:T(8,128)(2,1)} %cot_hbm.1) | copy-start | bytes 933892
  17.7 26.6 %copy-start.1 = (bf16[64,64]{1,0:T(8,128)(2,1)S(1)}, bf16[64,64]{1,0:T(8,128)(2,1)}, u32[]{:S(2)}) copy-start(bf16[64,64]{1,0:T(8,128)(2,1)} %w_scal_ref.3) | copy-start | bytes 24580
  17.7 26.5 %copy-start.2 = (bf16[32,32]{1,0:T(8,128)(2,1)S(1)}, bf16[32,32]{1,0:T(8,128)(2,1)}, u32[]{:S(2)}) copy-start(bf16[32,32]{1,0:T(8,128)(2,1)} %w_vec_ref.3) | copy-start | bytes 6148
  17.7 26.5 %copy-start.3 = (bf16[16,16]{1,0:T(8,128)(2,1)S(1)}, bf16[16,16]{1,0:T(8,128)(2,1)}, u32[]{:S(2)}) copy-start(bf16[16,16]{1,0:T(8,128)(2,1)} %w_ten_ref.3) | copy-start | bytes 1540
  17.8 26.5 %copy-start.4 = (bf16[144,128]{1,0:T(8,128)(2,1)S(1)}, bf16[144,128]{1,0:T(8,128)(2,1)}, u32[]{:S(2)}) copy-start(bf16[144,128]{1,0:T(8,128)(2,1)} %w_two_ref.1) | copy-start | bytes 110596
  17.8 26.5 %copy-start.6 = (s32[2048]{0:T(1024)S(1)}, s32[2048]{0:T(1024)}, u32[]{:S(2)}) copy-start(s32[2048]{0:T(1024)} %param.25) | copy-start | bytes 24580
  17.8 26.5 %copy-start.7 = (s32[2048]{0:T(1024)S(1)}, s32[2048]{0:T(1024)}, u32[]{:S(2)}) copy-start(s32[2048]{0:T(1024)} %param.26) | copy-start | bytes 24580
  17.8 26.5 %collective-permute-start.1 = (bf16[320,512]{1,0:T(8,128)(2,1)S(1)}, bf16[320,512]{1,0:T(8,128)(2,1)S(1)}, u32[]{:S(2)}, u32[]{:S(2)}) collective-permute-start(bf16[320,512]{1,0:T(8,128)(2,1)S(1)} %get-tuple-element.34.table_ref), channel_id=1, source_target_pairs={{0,7},{1,0},{2,1},{3,2},{4,3},{5,4},{6,5},{7,6},{8,15},{9,8},{10,9... | collective-permute-start | bytes 983048 | tf_op jit(solution)/shard_map/ppermute | solution.py:494
  18.5 25.8 %collective-permute-start = (bf16[320,512]{1,0:T(8,128)(2,1)S(1)}, bf16[320,512]{1,0:T(8,128)(2,1)S(1)}, u32[]{:S(2)}, u32[]{:S(2)}) collective-permute-start(bf16[320,512]{1,0:T(8,128)(2,1)S(1)} %get-tuple-element.34.table_ref), channel_id=1, source_target_pairs={{0,1},{1,2},{2,3},{3,4},{4,5},{5,6},{6,7},{7,0},{8,9},{9,10},{10,1... | collective-permute-start | bytes 983048 | tf_op jit(solution)/shard_map/ppermute | solution.py:494
  19.9 38.5 %all-to-all-start.1 = ((bf16[32,160,128]{2,1,0:T(8,128)(2,1)}), bf16[32,160,128]{2,1,0:T(8,128)(2,1)S(1)}, u32[]{:S(2)}, u32[]{:S(2)}) async-start(bf16[32,160,128]{2,1,0:T(8,128)(2,1)} %shard_map.225), calls=%async_computation.1 | async-start | bytes 2621440 | tf_op jit(solution)/shard_map/all_to_all | solution.py:481
  44.3 0.8 copy-start.5
  45.1 0.7 copy-start.8
  45.7 0.7 copy-start.9

commit v3 on v1

--- a/solution.py
+++ b/solution.py
@@ -186,8 +186,8 @@
 
 def mesh_kernel(
     table_ref,
-    low_ref,
-    high_ref,
+    inner_ref,
+    outer_ref,
     code_ref,
     cot_ref,
     w_one_ref,
@@ -216,8 +216,9 @@
 ):
     node_count = table_ref.shape[1]
     source_ref[:, :node_count] = table_ref[...]
-    low = low_ref[...]
-    high = high_ref[...]
+    even = lax.rem(lax.axis_index("sub"), 2) == 0
+    low = lax.cond(even, lambda: outer_ref[...], lambda: inner_ref[...])
+    high = lax.cond(even, lambda: inner_ref[...], lambda: outer_ref[...])
     source_ref[:, node_count : 2 * node_count] = dot(
         low, one_hot(join_index(low, FEAT + 3), node_count)
     ).astype(jnp.bfloat16)
@@ -484,9 +485,10 @@
     return jax.ShapeDtypeStruct(shape, dtype)
 
 
-def from_behind(shard, axis, by):
+def swapped(shard, axis, first):
     peers = lax.axis_size(axis)
-    return lax.ppermute(shard, axis, [(i, (i + by) % peers) for i in range(peers)])
+    pairs = [(at, (at + 1) % peers) for at in range(first, peers, 2)]
+    return lax.ppermute(shard, axis, pairs + [(there, here) for here, there in pairs])
 
 
 def on_device(
@@ -544,8 +546,8 @@
     )
     wanted = exchange(requests)
     wanted, table_late = lax.optimization_barrier((wanted, table))
-    low = from_behind(table_late, "sub", 1)
-    high = from_behind(table_late, "sub", -1)
+    inner = swapped(table_late, "sub", 0)
+    outer = swapped(table_late, "sub", 1)
     found = call(
         functools.partial(contact_gather_kernel, slot),
         pltpu.HBM((device_count, height, LANES), bf16),
@@ -594,8 +596,8 @@
         ),
     )(
         table,
-        low,
-        high,
+        inner,
+        outer,
         mesh_code,
         node_cot,
         w_one,

time: 80.5 us -> 80.5 us (level)
    all_to_all x1, waiting for transfers between devices: 2.66 us -> 1.81 us  [exchange(): return lax.all_to_all(blocks, axes, split_axis=0, concat_axis=0, tiled=True)]
  transfers between devices with their start and end apart: 3 -> 3, of which waited for: 2 -> 3; matrix products, arithmetic and copies ran while one was open for 0% -> 0% of each run, Pallas kernels for 13% -> 14%
where the time goes in v3:
time: 80.5 us; the launch traced here: 80.1 us
  blocking collectives  32.9 us (41%)
  waiting for transfers between devices  21.6 us (27%)
  Pallas kernels  16.6 us (21%)
  starting transfers between devices  5.69 us (7%)
  local copies, waits for them, and re-layouts  2.45 us (3%)
  between operations  0.84 us (1%)
    all_to_all x3, blocking collectives, exchange(): return lax.all_to_all(blocks, axes, split_axis=0, concat_axis=0, tiled=True)  32.9 us
    ppermute x2, waiting for transfers between devices, swapped(): lax.ppermute(shard, axis, pairs + [(there, here) for here, there in pairs])  19.8 us
    pallas_call x1, Pallas kernels, on_device(): call(mesh_kernel, (pltpu.HBM((FEAT, node_count), f32), pltpu.HBM((mesh_ro...  9.09 us
    all_to_all x1, starting transfers between devices, exchange(): return lax.all_to_all(blocks, axes, split_axis=0, concat_axis=0, tiled=True)  3.7 us
    pallas_call x1, Pallas kernels, on_device(): call(functools.partial(contact_kernel, slot, grad_scale), (shaped((FEAT,...  3.52 us
    unnamed x24, local copies, waits for them, and re-layouts  2.12 us
    ppermute x2, starting transfers between devices, swapped(): lax.ppermute(shard, axis, pairs + [(there, here) for here, there in pairs])  1.99 us
    all_to_all x1, waiting for transfers between devices, exchange(): return lax.all_to_all(blocks, axes, split_axis=0, concat_axis=0, tiled=True)  1.81 us
  transfers between devices with their start and end apart: 3, of which 3 were waited for; matrix products, arithmetic and copies ran while one was open for 0% of the time, Pallas kernels for 14%

profile of v3, /device:TPU:0, one launch (start us, length us, event | category | flops | bytes accessed | tf_op | source)
XLA Modules:
  0.0 80.1 jit_solution(8337460100658510529)
XLA Ops:
  0.6 1.0 %shard_map.224 = (bf16[320,512]{1,0:T(8,128)(2,1)S(1)}, s32[32,1,64]{2,1,0:T(1,128)S(1)}) custom-call(bf16[304,512]{1,0:T(8,128)(2,1)} %feat_ref.1, bf16[3,512]{1,0:T(4,128)(2,1)} %pos_ref.1, s32[1,512]{1,0:T(1,128)} %bitcast.16, s32[1,512]{1,0:T(1,128)} %bitcast.17, s32[16,128]{1,0:T(8,128)} %bitcast.15), custom_call_target="tpu_custom_call" | custom-call | tf_op jit(solution)/shard_map/pallas_call | solution.py:523
  1.7 14.2 %all_to_all.20.wanted_ref = s32[32,1,64]{2,1,0:T(1,128)S(1)} all-to-all(s32[32,1,64]{2,1,0:T(1,128)S(1)} %get-tuple-element.33), channel_id=1, replica_groups=mesh['dom'=4,'sub'=8] {'dom','sub'}, dimensions={0} | all-to-all | bytes 16384 | tf_op jit(solution)/shard_map/all_to_all | solution.py:477
  15.9 0.6 collective-permute-start.1
  16.5 1.4 %collective-permute-start = (bf16[320,512]{1,0:T(8,128)(2,1)S(1)}, bf16[320,512]{1,0:T(8,128)(2,1)S(1)}, u32[]{:S(2)}, u32[]{:S(2)}) collective-permute-start(bf16[320,512]{1,0:T(8,128)(2,1)S(1)} %get-tuple-element.36.table_ref), channel_id=1, source_target_pairs={{0,1},{2,3},{4,5},{6,7},{1,0},{3,2},{5,4},{7,6},{8,9},{10,11},{12,... | collective-permute-start | bytes 983048 | tf_op jit(solution)/shard_map/ppermute | solution.py:491
  17.9 1.8 %shard_map.225 = bf16[32,160,128]{2,1,0:T(8,128)(2,1)} custom-call(bf16[320,512]{1,0:T(8,128)(2,1)S(1)} %get-tuple-element.36.table_ref, s32[32,1,64]{2,1,0:T(1,128)S(1)} %all_to_all.20.wanted_ref), custom_call_target="tpu_custom_call" | custom-call | tf_op jit(solution)/shard_map/pallas_call | solution.py:551
  19.7 0.0 copy-start.10
  19.7 0.0 copy-start.11
  19.7 0.0 copy-start
  19.7 0.0 copy-start.1
  19.7 0.0 copy-start.2
  19.7 0.0 copy-start.3
  19.7 0.0 copy-start.4
  19.8 0.0 copy-start.6
  19.8 0.0 copy-start.7
  19.8 3.7 %all-to-all-start.1 = ((bf16[32,160,128]{2,1,0:T(8,128)(2,1)}), bf16[32,160,128]{2,1,0:T(8,128)(2,1)S(1)}, u32[]{:S(2)}, u32[]{:S(2)}) async-start(bf16[32,160,128]{2,1,0:T(8,128)(2,1)} %shard_map.225), calls=%async_computation.1 | async-start | bytes 2621440 | tf_op jit(solution)/shard_map/all_to_all | solution.py:477
  23.5 0.0 copy-done.10
  23.5 0.0 copy-done.11
  23.5 0.2 reshape.32
  23.7 0.1 copy.25
  23.9 4.4 %collective-permute-done.1.outer_ref = bf16[320,512]{1,0:T(8,128)(2,1)S(1)} collective-permute-done((bf16[320,512]{1,0:T(8,128)(2,1)S(1)}, bf16[320,512]{1,0:T(8,128)(2,1)S(1)}, u32[]{:S(2)}, u32[]{:S(2)}) %collective-permute-start.1) | collective-permute-done | bytes 327712 | tf_op jit(solution)/shard_map/ppermute | solution.py:491
  28.2 15.4 %collective-permute-done.inner_ref = bf16[320,512]{1,0:T(8,128)(2,1)S(1)} collective-permute-done((bf16[320,512]{1,0:T(8,128)(2,1)S(1)}, bf16[320,512]{1,0:T(8,128)(2,1)S(1)}, u32[]{:S(2)}, u32[]{:S(2)}) %collective-permute-start) | collective-permute-done | bytes 327712 | tf_op jit(solution)/shard_map/ppermute | solution.py:491
  43.7 0.0 copy-done
  43.7 0.0 copy-done.1
  43.7 0.0 copy-done.2
  43.7 0.0 copy-done.3
  43.7 0.0 copy-done.4
  43.7 0.0 copy-done.6
  43.7 0.0 copy-done.7
  43.7 0.0 copy-start.5
  43.7 0.7 copy-done.5
  44.5 0.0 copy-start.8
  44.5 0.7 copy-done.8
  45.1 0.0 copy-start.9
  45.1 0.7 copy-done.9
  45.8 9.1 %shard_map.226 = (f32[304,512]{1,0:T(8,128)}, f32[272,256]{1,0:T(8,128)}, bf16[1,384,1024]{2,1,0:T(8,128)(2,1)}, bf16[384,1024]{1,0:T(8,128)(2,1)S(1)}, s32[2,1,...) custom-call(bf16[320,512]{1,0:T(8,128)(2,1)S(1)} %get-tuple-element.36.table_ref, ...), custom_call_target="tpu_custom_call" | custom-call | flops 40000000000 | bytes 8000000 | tf_op jit(solution)/shard_map/pallas_call | solution.py:572
  54.9 1.8 %all-to-all-done.1.reply_ref = bf16[32,160,128]{2,1,0:T(8,128)(2,1)S(1)} async-done(((bf16[32,160,128]{2,1,0:T(8,128)(2,1)}), bf16[32,160,128]{2,1,0:T(8,128)(2,1)S(1)}, u32[]{:S(2)}, u32[]{:S(2)}) %all-to-all-start.1) | async-done | bytes 1310752 | tf_op jit(solution)/shard_map/all_to_all | solution.py:477
  56.7 3.5 %shard_map.227 = (bf16[304,512]{1,0:T(8,128)(2,1)S(1)}, bf16[32,5,2,128]{3,2,1,0:T(2,128)(2,1)S(1)}) custom-call(bf16[32,160,128]{2,1,0:T(8,128)(2,1)S(1)} %all-to-all-done.1.reply_ref, bf16[384,1024]{1,0:T(8,128)(2,1)S(1)} %get-tuple-element.39.first_ref, s32[2,1,1024]{2,1,0:T(1,128)S(1)} %get-tuple-element.40.code_ref, ...), custom_call_target="tpu_custom_call" | custom-call | tf_op jit(solution)/shard_map/pallas_call | solution.py:616
  60.2 9.6 %all_to_all.21.parts_ref = bf16[32,5,2,128]{3,2,1,0:T(2,128)(2,1)S(1)} all-to-all(bf16[32,5,2,128]{3,2,1,0:T(2,128)(2,1)S(1)} %get-tuple-element.46), channel_id=1, replica_groups=mesh['dom'=4,'sub'=8] {'dom','sub'}, dimensions={0} | all-to-all | bytes 163840 | tf_op jit(solution)/shard_map/all_to_all | solution.py:477
  69.8 0.1 shard_map.228
  69.9 9.1 %all_to_all.22.blocks_ref = bf16[32,5,2,128]{3,2,1,0:T(2,128)(2,1)S(1)} all-to-all(bf16[32,5,2,128]{3,2,1,0:T(2,128)(2,1)S(1)} %shard_map.228), channel_id=1, replica_groups=mesh['dom'=4,'sub'=8] {'dom','sub'}, dimensions={0} | all-to-all | bytes 163840 | tf_op jit(solution)/shard_map/all_to_all | solution.py:477
  79.0 1.1 %shard_map.229 = (bf16[304,512]{1,0:T(8,128)(2,1)}, f32[128,128]{1,0:T(8,128)}, f32[1,128]{1,0:T(1,128)}, f32[1,128]{1,0:T(1,128)}, f32[144,128]{1,0:T(8,128)}, ...) custom-call(bf16[32,5,2,128]{3,2,1,0:T(2,128)(2,1)S(1)} %all_to_all.22.blocks_ref, ...), custom_call_target="tpu_custom_call" | custom-call | tf_op jit(solution)/shard_map/pallas_call | solution.py:639
  (2 shorter events, 0.0 us)
Async XLA Ops:
  15.9 12.3 %collective-permute-start.1 = (bf16[320,512]{1,0:T(8,128)(2,1)S(1)}, bf16[320,512]{1,0:T(8,128)(2,1)S(1)}, u32[]{:S(2)}, u32[]{:S(2)}) collective-permute-start(bf16[320,512]{1,0:T(8,128)(2,1)S(1)} %get-tuple-element.36.table_ref), channel_id=1, source_target_pairs={{1,2},{3,4},{5,6},{7,0},{2,1},{4,3},{6,5},{0,7},{9,10},{11,12},{13... | collective-permute-start | bytes 983048 | tf_op jit(solution)/shard_map/ppermute | solution.py:491
  16.5 27.1 %collective-permute-start = (bf16[320,512]{1,0:T(8,128)(2,1)S(1)}, bf16[320,512]{1,0:T(8,128)(2,1)S(1)}, u32[]{:S(2)}, u32[]{:S(2)}) collective-permute-start(bf16[320,512]{1,0:T(8,128)(2,1)S(1)} %get-tuple-element.36.table_ref), channel_id=1, source_target_pairs={{0,1},{2,3},{4,5},{6,7},{1,0},{3,2},{5,4},{7,6},{8,9},{10,11},{12,... | collective-permute-start | bytes 983048 | tf_op jit(solution)/shard_map/ppermute | solution.py:491
  19.7 3.8 %copy-start.10 = (s32[3072]{0:T(1024)S(1)}, s32[3072]{0:T(1024)}, u32[]{:S(2)}) copy-start(s32[3072]{0:T(1024)} %param.20) | copy-start | bytes 36868
  19.7 3.8 %copy-start.11 = (s32[3072]{0:T(1024)S(1)}, s32[3072]{0:T(1024)}, u32[]{:S(2)}) copy-start(s32[3072]{0:T(1024)} %param.21) | copy-start | bytes 36868
  19.7 24.0 %copy-start = (bf16[304,512]{1,0:T(8,128)(2,1)S(1)}, bf16[304,512]{1,0:T(8,128)(2,1)}, u32[]{:S(2)}) copy-start(bf16[304,512]{1,0:T(8,128)(2,1)} %cot_hbm.1) | copy-start | bytes 933892
  19.7 24.0 %copy-start.1 = (bf16[64,64]{1,0:T(8,128)(2,1)S(1)}, bf16[64,64]{1,0:T(8,128)(2,1)}, u32[]{:S(2)}) copy-start(bf16[64,64]{1,0:T(8,128)(2,1)} %w_scal_ref.3) | copy-start | bytes 24580
  19.7 23.9 %copy-start.2 = (bf16[32,32]{1,0:T(8,128)(2,1)S(1)}, bf16[32,32]{1,0:T(8,128)(2,1)}, u32[]{:S(2)}) copy-start(bf16[32,32]{1,0:T(8,128)(2,1)} %w_vec_ref.3) | copy-start | bytes 6148
  19.7 23.9 %copy-start.3 = (bf16[16,16]{1,0:T(8,128)(2,1)S(1)}, bf16[16,16]{1,0:T(8,128)(2,1)}, u32[]{:S(2)}) copy-start(bf16[16,16]{1,0:T(8,128)(2,1)} %w_ten_ref.3) | copy-start | bytes 1540
  19.7 23.9 %copy-start.4 = (bf16[144,128]{1,0:T(8,128)(2,1)S(1)}, bf16[144,128]{1,0:T(8,128)(2,1)}, u32[]{:S(2)}) copy-start(bf16[144,128]{1,0:T(8,128)(2,1)} %w_two_ref.1) | copy-start | bytes 110596
  19.8 23.9 %copy-start.6 = (s32[2048]{0:T(1024)S(1)}, s32[2048]{0:T(1024)}, u32[]{:S(2)}) copy-start(s32[2048]{0:T(1024)} %param.25) | copy-start | bytes 24580
  19.8 23.9 %copy-start.7 = (s32[2048]{0:T(1024)S(1)}, s32[2048]{0:T(1024)}, u32[]{:S(2)}) copy-start(s32[2048]{0:T(1024)} %param.26) | copy-start | bytes 24580
  19.8 36.9 %all-to-all-start.1 = ((bf16[32,160,128]{2,1,0:T(8,128)(2,1)}), bf16[32,160,128]{2,1,0:T(8,128)(2,1)S(1)}, u32[]{:S(2)}, u32[]{:S(2)}) async-start(bf16[32,160,128]{2,1,0:T(8,128)(2,1)} %shard_map.225), calls=%async_computation.1 | async-start | bytes 2621440 | tf_op jit(solution)/shard_map/all_to_all | solution.py:477
  43.7 0.8 copy-start.5
  44.5 0.7 copy-start.8
  45.1 0.7 copy-start.9

commit v4 on v3

--- a/solution.py
+++ b/solution.py
@@ -117,17 +117,30 @@
         copy.wait()
 
 
-def edge_math(src, base, first, inputs, pos_recv, back, live, weights):
+def edge_math(*operands):
+    steps = edge_steps(*operands)
+    while True:
+        try:
+            next(steps)
+        except StopIteration as end:
+            return end.value
+
+
+def edge_steps(src, base, w_first, first, inputs, pos_recv, back, live, weights):
     w_dist, w_two, w_two_t = weights
     edges = src.shape[1]
     offset = src[FEAT : FEAT + 3] - pos_recv
     if live is not None:
         offset = offset * live
     distance = jnp.sum(offset * offset, 0, keepdims=True)
-    linear = base + first + w_dist * distance
+    product = dot(w_first, first)
+    yield
+    linear = base + product + w_dist * distance
     squashed = 0.5 * jnp.tanh(0.5 * linear) + 0.5
     hidden = (linear * squashed).astype(jnp.bfloat16)
+    yield
     gates = dot(w_two, hidden)
+    yield
     gate_vec = gates[CS : CS + CV]
     gate_dir = gates[CS + CV : CS + 2 * CV]
     gate_ten = gates[CS + 2 * CV :]
@@ -148,7 +161,10 @@
     dgates = jnp.concatenate([back[:CS] * src[:CS], vec_part, dir_part, ten_part], 0).astype(
         jnp.bfloat16
     )
+    message = message.astype(jnp.bfloat16) if live is None else message
+    yield
     hidden_grad = dot(w_two_t, dgates)
+    yield
     linear_grad = (hidden_grad * squashed * (1.0 + linear * (1.0 - squashed))).astype(jnp.bfloat16)
     rows = lax.broadcasted_iota(jnp.int32, (16, edges), 0)
     coarse = distance.astype(jnp.bfloat16).astype(jnp.float32)
@@ -246,7 +262,7 @@
         scal_send = src[:CS].astype(jnp.bfloat16)
         inputs = jnp.concatenate([scal_recv, scal_send], 0)
         message, grads = edge_math(
-            src, recv_linear, dot(w_one[:, CS:], scal_send), inputs, pos_recv, back, live, weights
+            src, recv_linear, w_one[:, CS:], scal_send, inputs, pos_recv, back, live, weights
         )
         agg_ref[...] += message
         add_grads(grads_ref, grads)
@@ -324,32 +340,37 @@
     w_two = layers_ref[HID:]
     b_column, dist_column = as_columns(rows_ref[0:1], rows_ref[1:2])
     weights = (dist_column, w_two, w_two.T)
-    for chunk in range(chunks):
+    def steps_of(chunk):
         src_rows = src_scr[chunk]
-        if chunk == 1:
-            for copy in copies:
-                copy.wait()
         recv = first_ref[...] if chunk == 0 else recv_ref[chunk - 1]
         inputs = jnp.concatenate([recv[FEAT + 16 :], src_rows[:CS]], 0)
-        message, grads = edge_math(
+        message, grads = yield from edge_steps(
             src_rows.astype(jnp.float32),
             b_column,
-            dot(w_one, inputs),
+            w_one,
+            inputs,
             inputs,
             recv[FEAT : FEAT + 16].astype(jnp.float32)[:3],
             recv[:FEAT].astype(jnp.float32),
             None,
             weights,
         )
-        scattered = dot(message.astype(jnp.bfloat16), one_hot(code_ref[chunk], node_count), 1, 1)
-        if chunk == 0:
-            held = (scattered, grads)
-            continue
-        agg_ref[...] += scattered
-        add_grads(grads_ref, grads)
-        if chunk == 1:
-            agg_ref[...] += held[0]
-            add_grads(grads_ref, held[1])
+        yield
+        return dot(message, one_hot(code_ref[chunk], node_count), 1, 1), grads
+
+    running = [steps_of(0)]
+    next(running[0])
+    for copy in copies:
+        copy.wait()
+    running += [steps_of(chunk) for chunk in range(1, chunks)]
+    while running:
+        for steps in list(running):
+            try:
+                next(steps)
+            except StopIteration as end:
+                agg_ref[...] += end.value[0]
+                add_grads(grads_ref, end.value[1])
+                running.remove(steps)
     agg_rows = agg_ref[...].astype(jnp.bfloat16)
     agg_out_ref[...] = agg_rows
     cot = cot_ref[...]

time: 80.5 us -> 81.5 us (1.012)
  Pallas kernels: 16.6 us -> 17.6 us
    pallas_call x1, Pallas kernels: 3.52 us -> 4.53 us  [on_device(): call(functools.partial(contact_kernel, slot, grad_scale), (shaped((FEAT,...]
  transfers between devices with their start and end apart: 3 -> 3, of which waited for: 3 -> 3; matrix products, arithmetic and copies ran while one was open for 0% -> 0% of each run, Pallas kernels for 14% -> 13%
where the time goes in v4:
time: 81.5 us; the launch traced here: 81.1 us
  blocking collectives  32.9 us (40%)
  waiting for transfers between devices  21.6 us (27%)
  Pallas kernels  17.6 us (22%)
  starting transfers between devices  5.69 us (7%)
  local copies, waits for them, and re-layouts  2.45 us (3%)
  between operations  0.84 us (1%)
    all_to_all x3, blocking collectives, exchange(): return lax.all_to_all(blocks, axes, split_axis=0, concat_axis=0, tiled=True)  32.9 us
    ppermute x2, waiting for transfers between devices, swapped(): lax.ppermute(shard, axis, pairs + [(there, here) for here, there in pairs])  19.8 us
    pallas_call x1, Pallas kernels, on_device(): call(mesh_kernel, (pltpu.HBM((FEAT, node_count), f32), pltpu.HBM((mesh_ro...  9.09 us
    pallas_call x1, Pallas kernels, on_device(): call(functools.partial(contact_kernel, slot, grad_scale), (shaped((FEAT,...  4.53 us
    all_to_all x1, starting transfers between devices, exchange(): return lax.all_to_all(blocks, axes, split_axis=0, concat_axis=0, tiled=True)  3.7 us
    unnamed x24, local copies, waits for them, and re-layouts  2.12 us
    ppermute x2, starting transfers between devices, swapped(): lax.ppermute(shard, axis, pairs + [(there, here) for here, there in pairs])  1.99 us
    all_to_all x1, waiting for transfers between devices, exchange(): return lax.all_to_all(blocks, axes, split_axis=0, concat_axis=0, tiled=True)  1.81 us
  transfers between devices with their start and end apart: 3, of which 3 were waited for; matrix products, arithmetic and copies ran while one was open for 0% of the time, Pallas kernels for 13%

profile of v4, /device:TPU:0, one launch (start us, length us, event | category | flops | bytes accessed | tf_op | source)
XLA Modules:
  0.0 81.1 jit_solution(4140243756973950412)
XLA Ops:
  0.6 1.0 %shard_map.224 = (bf16[320,512]{1,0:T(8,128)(2,1)S(1)}, s32[32,1,64]{2,1,0:T(1,128)S(1)}) custom-call(bf16[304,512]{1,0:T(8,128)(2,1)} %feat_ref.1, bf16[3,512]{1,0:T(4,128)(2,1)} %pos_ref.1, s32[1,512]{1,0:T(1,128)} %bitcast.16, s32[1,512]{1,0:T(1,128)} %bitcast.17, s32[16,128]{1,0:T(8,128)} %bitcast.15), custom_call_target="tpu_custom_call" | custom-call | tf_op jit(solution)/shard_map/pallas_call | solution.py:544
  1.7 14.2 %all_to_all.20.wanted_ref = s32[32,1,64]{2,1,0:T(1,128)S(1)} all-to-all(s32[32,1,64]{2,1,0:T(1,128)S(1)} %get-tuple-element.33), channel_id=1, replica_groups=mesh['dom'=4,'sub'=8] {'dom','sub'}, dimensions={0} | all-to-all | bytes 16384 | tf_op jit(solution)/shard_map/all_to_all | solution.py:498
  15.9 0.6 collective-permute-start.1
  16.5 1.4 %collective-permute-start = (bf16[320,512]{1,0:T(8,128)(2,1)S(1)}, bf16[320,512]{1,0:T(8,128)(2,1)S(1)}, u32[]{:S(2)}, u32[]{:S(2)}) collective-permute-start(bf16[320,512]{1,0:T(8,128)(2,1)S(1)} %get-tuple-element.36.table_ref), channel_id=1, source_target_pairs={{0,1},{2,3},{4,5},{6,7},{1,0},{3,2},{5,4},{7,6},{8,9},{10,11},{12,... | collective-permute-start | bytes 983048 | tf_op jit(solution)/shard_map/ppermute | solution.py:512
  17.9 1.8 %shard_map.225 = bf16[32,160,128]{2,1,0:T(8,128)(2,1)} custom-call(bf16[320,512]{1,0:T(8,128)(2,1)S(1)} %get-tuple-element.36.table_ref, s32[32,1,64]{2,1,0:T(1,128)S(1)} %all_to_all.20.wanted_ref), custom_call_target="tpu_custom_call" | custom-call | tf_op jit(solution)/shard_map/pallas_call | solution.py:572
  19.7 0.0 copy-start.10
  19.7 0.0 copy-start.11
  19.7 0.0 copy-start
  19.7 0.0 copy-start.1
  19.7 0.0 copy-start.2
  19.7 0.0 copy-start.3
  19.7 0.0 copy-start.4
  19.8 0.0 copy-start.6
  19.8 0.0 copy-start.7
  19.8 3.7 %all-to-all-start.1 = ((bf16[32,160,128]{2,1,0:T(8,128)(2,1)}), bf16[32,160,128]{2,1,0:T(8,128)(2,1)S(1)}, u32[]{:S(2)}, u32[]{:S(2)}) async-start(bf16[32,160,128]{2,1,0:T(8,128)(2,1)} %shard_map.225), calls=%async_computation.1 | async-start | bytes 2621440 | tf_op jit(solution)/shard_map/all_to_all | solution.py:498
  23.5 0.0 copy-done.10
  23.5 0.0 copy-done.11
  23.5 0.2 reshape.32
  23.7 0.1 copy.25
  23.9 4.4 %collective-permute-done.1.outer_ref = bf16[320,512]{1,0:T(8,128)(2,1)S(1)} collective-permute-done((bf16[320,512]{1,0:T(8,128)(2,1)S(1)}, bf16[320,512]{1,0:T(8,128)(2,1)S(1)}, u32[]{:S(2)}, u32[]{:S(2)}) %collective-permute-start.1) | collective-permute-done | bytes 327712 | tf_op jit(solution)/shard_map/ppermute | solution.py:512
  28.2 15.4 %collective-permute-done.inner_ref = bf16[320,512]{1,0:T(8,128)(2,1)S(1)} collective-permute-done((bf16[320,512]{1,0:T(8,128)(2,1)S(1)}, bf16[320,512]{1,0:T(8,128)(2,1)S(1)}, u32[]{:S(2)}, u32[]{:S(2)}) %collective-permute-start) | collective-permute-done | bytes 327712 | tf_op jit(solution)/shard_map/ppermute | solution.py:512
  43.7 0.0 copy-done
  43.7 0.0 copy-done.1
  43.7 0.0 copy-done.2
  43.7 0.0 copy-done.3
  43.7 0.0 copy-done.4
  43.7 0.0 copy-done.6
  43.7 0.0 copy-done.7
  43.7 0.0 copy-start.5
  43.7 0.7 copy-done.5
  44.5 0.0 copy-start.8
  44.5 0.7 copy-done.8
  45.1 0.0 copy-start.9
  45.1 0.7 copy-done.9
  45.8 9.1 %shard_map.226 = (f32[304,512]{1,0:T(8,128)}, f32[272,256]{1,0:T(8,128)}, bf16[1,384,1024]{2,1,0:T(8,128)(2,1)}, bf16[384,1024]{1,0:T(8,128)(2,1)S(1)}, s32[2,1,...) custom-call(bf16[320,512]{1,0:T(8,128)(2,1)S(1)} %get-tuple-element.36.table_ref, ...), custom_call_target="tpu_custom_call" | custom-call | flops 40000000000 | bytes 8000000 | tf_op jit(solution)/shard_map/pallas_call | solution.py:593
  54.9 1.8 %all-to-all-done.1.reply_ref = bf16[32,160,128]{2,1,0:T(8,128)(2,1)S(1)} async-done(((bf16[32,160,128]{2,1,0:T(8,128)(2,1)}), bf16[32,160,128]{2,1,0:T(8,128)(2,1)S(1)}, u32[]{:S(2)}, u32[]{:S(2)}) %all-to-all-start.1) | async-done | bytes 1310752 | tf_op jit(solution)/shard_map/all_to_all | solution.py:498
  56.7 4.5 %shard_map.227 = (bf16[304,512]{1,0:T(8,128)(2,1)S(1)}, bf16[32,5,2,128]{3,2,1,0:T(2,128)(2,1)S(1)}) custom-call(bf16[32,160,128]{2,1,0:T(8,128)(2,1)S(1)} %all-to-all-done.1.reply_ref, bf16[384,1024]{1,0:T(8,128)(2,1)S(1)} %get-tuple-element.39.first_ref, s32[2,1,1024]{2,1,0:T(1,128)S(1)} %get-tuple-element.40.code_ref, ...), custom_call_target="tpu_custom_call" | custom-call | tf_op jit(solution)/shard_map/pallas_call | solution.py:637
  61.2 9.6 %all_to_all.21.parts_ref = bf16[32,5,2,128]{3,2,1,0:T(2,128)(2,1)S(1)} all-to-all(bf16[32,5,2,128]{3,2,1,0:T(2,128)(2,1)S(1)} %get-tuple-element.46), channel_id=1, replica_groups=mesh['dom'=4,'sub'=8] {'dom','sub'}, dimensions={0} | all-to-all | bytes 163840 | tf_op jit(solution)/shard_map/all_to_all | solution.py:498
  70.8 0.1 shard_map.228
  70.9 9.1 %all_to_all.22.blocks_ref = bf16[32,5,2,128]{3,2,1,0:T(2,128)(2,1)S(1)} all-to-all(bf16[32,5,2,128]{3,2,1,0:T(2,128)(2,1)S(1)} %shard_map.228), channel_id=1, replica_groups=mesh['dom'=4,'sub'=8] {'dom','sub'}, dimensions={0} | all-to-all | bytes 163840 | tf_op jit(solution)/shard_map/all_to_all | solution.py:498
  80.0 1.1 %shard_map.229 = (bf16[304,512]{1,0:T(8,128)(2,1)}, f32[128,128]{1,0:T(8,128)}, f32[1,128]{1,0:T(1,128)}, f32[1,128]{1,0:T(1,128)}, f32[144,128]{1,0:T(8,128)}, ...) custom-call(bf16[32,5,2,128]{3,2,1,0:T(2,128)(2,1)S(1)} %all_to_all.22.blocks_ref, ...), custom_call_target="tpu_custom_call" | custom-call | tf_op jit(solution)/shard_map/pallas_call | solution.py:660
  (2 shorter events, 0.0 us)
Async XLA Ops:
  15.9 12.3 %collective-permute-start.1 = (bf16[320,512]{1,0:T(8,128)(2,1)S(1)}, bf16[320,512]{1,0:T(8,128)(2,1)S(1)}, u32[]{:S(2)}, u32[]{:S(2)}) collective-permute-start(bf16[320,512]{1,0:T(8,128)(2,1)S(1)} %get-tuple-element.36.table_ref), channel_id=1, source_target_pairs={{1,2},{3,4},{5,6},{7,0},{2,1},{4,3},{6,5},{0,7},{9,10},{11,12},{13... | collective-permute-start | bytes 983048 | tf_op jit(solution)/shard_map/ppermute | solution.py:512
  16.5 27.1 %collective-permute-start = (bf16[320,512]{1,0:T(8,128)(2,1)S(1)}, bf16[320,512]{1,0:T(8,128)(2,1)S(1)}, u32[]{:S(2)}, u32[]{:S(2)}) collective-permute-start(bf16[320,512]{1,0:T(8,128)(2,1)S(1)} %get-tuple-element.36.table_ref), channel_id=1, source_target_pairs={{0,1},{2,3},{4,5},{6,7},{1,0},{3,2},{5,4},{7,6},{8,9},{10,11},{12,... | collective-permute-start | bytes 983048 | tf_op jit(solution)/shard_map/ppermute | solution.py:512
  19.7 3.8 %copy-start.10 = (s32[3072]{0:T(1024)S(1)}, s32[3072]{0:T(1024)}, u32[]{:S(2)}) copy-start(s32[3072]{0:T(1024)} %param.20) | copy-start | bytes 36868
  19.7 3.8 %copy-start.11 = (s32[3072]{0:T(1024)S(1)}, s32[3072]{0:T(1024)}, u32[]{:S(2)}) copy-start(s32[3072]{0:T(1024)} %param.21) | copy-start | bytes 36868
  19.7 24.0 %copy-start = (bf16[304,512]{1,0:T(8,128)(2,1)S(1)}, bf16[304,512]{1,0:T(8,128)(2,1)}, u32[]{:S(2)}) copy-start(bf16[304,512]{1,0:T(8,128)(2,1)} %cot_hbm.1) | copy-start | bytes 933892
  19.7 24.0 %copy-start.1 = (bf16[64,64]{1,0:T(8,128)(2,1)S(1)}, bf16[64,64]{1,0:T(8,128)(2,1)}, u32[]{:S(2)}) copy-start(bf16[64,64]{1,0:T(8,128)(2,1)} %w_scal_ref.3) | copy-start | bytes 24580
  19.7 23.9 %copy-start.2 = (bf16[32,32]{1,0:T(8,128)(2,1)S(1)}, bf16[32,32]{1,0:T(8,128)(2,1)}, u32[]{:S(2)}) copy-start(bf16[32,32]{1,0:T(8,128)(2,1)} %w_vec_ref.3) | copy-start | bytes 6148
  19.7 23.9 %copy-start.3 = (bf16[16,16]{1,0:T(8,128)(2,1)S(1)}, bf16[16,16]{1,0:T(8,128)(2,1)}, u32[]{:S(2)}) copy-start(bf16[16,16]{1,0:T(8,128)(2,1)} %w_ten_ref.3) | copy-start | bytes 1540
  19.7 23.9 %copy-start.4 = (bf16[144,128]{1,0:T(8,128)(2,1)S(1)}, bf16[144,128]{1,0:T(8,128)(2,1)}, u32[]{:S(2)}) copy-start(bf16[144,128]{1,0:T(8,128)(2,1)} %w_two_ref.1) | copy-start | bytes 110596
  19.8 23.9 %copy-start.6 = (s32[2048]{0:T(1024)S(1)}, s32[2048]{0:T(1024)}, u32[]{:S(2)}) copy-start(s32[2048]{0:T(1024)} %param.25) | copy-start | bytes 24580
  19.8 23.9 %copy-start.7 = (s32[2048]{0:T(1024)S(1)}, s32[2048]{0:T(1024)}, u32[]{:S(2)}) copy-start(s32[2048]{0:T(1024)} %param.26) | copy-start | bytes 24580
  19.8 36.9 %all-to-all-start.1 = ((bf16[32,160,128]{2,1,0:T(8,128)(2,1)}), bf16[32,160,128]{2,1,0:T(8,128)(2,1)S(1)}, u32[]{:S(2)}, u32[]{:S(2)}) async-start(bf16[32,160,128]{2,1,0:T(8,128)(2,1)} %shard_map.225), calls=%async_computation.1 | async-start | bytes 2621440 | tf_op jit(solution)/shard_map/all_to_all | solution.py:498
  43.7 0.8 copy-start.5
  44.5 0.7 copy-start.8
  45.1 0.7 copy-start.9

commit v5 on v3

--- a/solution.py
+++ b/solution.py
@@ -119,8 +119,10 @@
 
 def edge_math(src, base, first, inputs, pos_recv, back, live, weights):
     w_dist, w_two, w_two_t = weights
-    edges = src.shape[1]
-    offset = src[FEAT : FEAT + 3] - pos_recv
+    edges = inputs.shape[1]
+    bf16 = jnp.bfloat16
+    kept = jnp.float32 if live is not None else bf16
+    offset = src(slice(FEAT, ROWS))[:3] - pos_recv
     if live is not None:
         offset = offset * live
     distance = jnp.sum(offset * offset, 0, keepdims=True)
@@ -131,23 +133,26 @@
     gate_vec = gates[CS : CS + CV]
     gate_dir = gates[CS + CV : CS + 2 * CV]
     gate_ten = gates[CS + 2 * CV :]
-    message = [gates[:CS] * src[:CS]]
+    scal = src(slice(0, CS))
+    message = [(gates[:CS] * scal).astype(kept)]
+    dgates = [(back(slice(0, CS)) * scal).astype(bf16)]
     vec_part = jnp.zeros((CV, edges), jnp.float32)
     dir_part = jnp.zeros((CV, edges), jnp.float32)
     for k in range(3):
         rows = slice(CS + k * CV, CS + (k + 1) * CV)
-        message.append(gate_vec * src[rows] + gate_dir * offset[k : k + 1])
-        vec_part = vec_part + back[rows] * src[rows]
-        dir_part = dir_part + back[rows] * offset[k : k + 1]
+        sent, pull = src(rows), back(rows)
+        message.append((gate_vec * sent + gate_dir * offset[k : k + 1]).astype(kept))
+        vec_part = vec_part + pull * sent
+        dir_part = dir_part + pull * offset[k : k + 1]
     ten_part = jnp.zeros((CT, edges), jnp.float32)
     for m in range(9):
         rows = slice(CS + 3 * CV + m * CT, CS + 3 * CV + (m + 1) * CT)
-        message.append(gate_ten * src[rows])
-        ten_part = ten_part + back[rows] * src[rows]
+        sent = src(rows)
+        message.append((gate_ten * sent).astype(kept))
+        ten_part = ten_part + back(rows) * sent
     message = jnp.concatenate(message, 0)
-    dgates = jnp.concatenate([back[:CS] * src[:CS], vec_part, dir_part, ten_part], 0).astype(
-        jnp.bfloat16
-    )
+    dgates += [part.astype(bf16) for part in (vec_part, dir_part, ten_part)]
+    dgates = jnp.concatenate(dgates, 0)
     hidden_grad = dot(w_two_t, dgates)
     linear_grad = (hidden_grad * squashed * (1.0 + linear * (1.0 - squashed))).astype(jnp.bfloat16)
     rows = lax.broadcasted_iota(jnp.int32, (16, edges), 0)
@@ -242,11 +247,17 @@
         code = code_ref[step]
         src = dot(source_ref[...], one_hot(code, 3 * node_count))
         live = jnp.where(code >= 0, 1.0, 0.0)
-        back = receive_ref[:FEAT].astype(jnp.float32)
         scal_send = src[:CS].astype(jnp.bfloat16)
         inputs = jnp.concatenate([scal_recv, scal_send], 0)
         message, grads = edge_math(
-            src, recv_linear, dot(w_one[:, CS:], scal_send), inputs, pos_recv, back, live, weights
+            lambda rows: src[rows],
+            recv_linear,
+            dot(w_one[:, CS:], scal_send),
+            inputs,
+            pos_recv,
+            lambda rows: receive_ref[rows].astype(jnp.float32),
+            live,
+            weights,
         )
         agg_ref[...] += message
         add_grads(grads_ref, grads)
@@ -325,23 +336,22 @@
     b_column, dist_column = as_columns(rows_ref[0:1], rows_ref[1:2])
     weights = (dist_column, w_two, w_two.T)
     for chunk in range(chunks):
-        src_rows = src_scr[chunk]
         if chunk == 1:
             for copy in copies:
                 copy.wait()
-        recv = first_ref[...] if chunk == 0 else recv_ref[chunk - 1]
-        inputs = jnp.concatenate([recv[FEAT + 16 :], src_rows[:CS]], 0)
+        recv = first_ref if chunk == 0 else recv_ref.at[chunk - 1]
+        inputs = jnp.concatenate([recv[FEAT + 16 :], src_scr[chunk, :CS]], 0)
         message, grads = edge_math(
-            src_rows.astype(jnp.float32),
+            lambda rows: src_scr[chunk, rows].astype(jnp.float32),
             b_column,
             dot(w_one, inputs),
             inputs,
             recv[FEAT : FEAT + 16].astype(jnp.float32)[:3],
-            recv[:FEAT].astype(jnp.float32),
+            lambda rows: recv[rows].astype(jnp.float32),
             None,
             weights,
         )
-        scattered = dot(message.astype(jnp.bfloat16), one_hot(code_ref[chunk], node_count), 1, 1)
+        scattered = dot(message, one_hot(code_ref[chunk], node_count), 1, 1)
         if chunk == 0:
             held = (scattered, grads)
             continue

time: 80.5 us -> 80.5 us (level)
  no operation moved by 1% of the time
where the time goes in v5:
time: 80.5 us; the launch traced here: 80.1 us
  blocking collectives  32.9 us (41%)
  waiting for transfers between devices  21.6 us (27%)
  Pallas kernels  16.6 us (21%)
  starting transfers between devices  5.69 us (7%)
  local copies, waits for them, and re-layouts  2.45 us (3%)
  between operations  0.84 us (1%)
    all_to_all x3, blocking collectives, exchange(): return lax.all_to_all(blocks, axes, split_axis=0, concat_axis=0, tiled=True)  32.9 us
    ppermute x2, waiting for transfers between devices, swapped(): lax.ppermute(shard, axis, pairs + [(there, here) for here, there in pairs])  19.8 us
    pallas_call x1, Pallas kernels, on_device(): call(mesh_kernel, (pltpu.HBM((FEAT, node_count), f32), pltpu.HBM((mesh_ro...  9.09 us
    all_to_all x1, starting transfers between devices, exchange(): return lax.all_to_all(blocks, axes, split_axis=0, concat_axis=0, tiled=True)  3.7 us
    pallas_call x1, Pallas kernels, on_device(): call(functools.partial(contact_kernel, slot, grad_scale), (shaped((FEAT,...  3.51 us
    unnamed x24, local copies, waits for them, and re-layouts  2.12 us
    ppermute x2, starting transfers between devices, swapped(): lax.ppermute(shard, axis, pairs + [(there, here) for here, there in pairs])  1.99 us
    all_to_all x1, waiting for transfers between devices, exchange(): return lax.all_to_all(blocks, axes, split_axis=0, concat_axis=0, tiled=True)  1.81 us
  transfers between devices with their start and end apart: 3, of which 3 were waited for; matrix products, arithmetic and copies ran while one was open for 0% of the time, Pallas kernels for 14%

profile of v5, /device:TPU:0, one launch (start us, length us, event | category | flops | bytes accessed | tf_op | source)
XLA Modules:
  0.0 80.1 jit_solution(1141074147180830951)
XLA Ops:
  0.6 1.0 %shard_map.224 = (bf16[320,512]{1,0:T(8,128)(2,1)S(1)}, s32[32,1,64]{2,1,0:T(1,128)S(1)}) custom-call(bf16[304,512]{1,0:T(8,128)(2,1)} %feat_ref.1, bf16[3,512]{1,0:T(4,128)(2,1)} %pos_ref.1, s32[1,512]{1,0:T(1,128)} %bitcast.16, s32[1,512]{1,0:T(1,128)} %bitcast.17, s32[16,128]{1,0:T(8,128)} %bitcast.15), custom_call_target="tpu_custom_call" | custom-call | tf_op jit(solution)/shard_map/pallas_call | solution.py:533
  1.7 14.2 %all_to_all.20.wanted_ref = s32[32,1,64]{2,1,0:T(1,128)S(1)} all-to-all(s32[32,1,64]{2,1,0:T(1,128)S(1)} %get-tuple-element.33), channel_id=1, replica_groups=mesh['dom'=4,'sub'=8] {'dom','sub'}, dimensions={0} | all-to-all | bytes 16384 | tf_op jit(solution)/shard_map/all_to_all | solution.py:487
  15.9 0.6 collective-permute-start.1
  16.5 1.4 %collective-permute-start = (bf16[320,512]{1,0:T(8,128)(2,1)S(1)}, bf16[320,512]{1,0:T(8,128)(2,1)S(1)}, u32[]{:S(2)}, u32[]{:S(2)}) collective-permute-start(bf16[320,512]{1,0:T(8,128)(2,1)S(1)} %get-tuple-element.36.table_ref), channel_id=1, source_target_pairs={{0,1},{2,3},{4,5},{6,7},{1,0},{3,2},{5,4},{7,6},{8,9},{10,11},{12,... | collective-permute-start | bytes 983048 | tf_op jit(solution)/shard_map/ppermute | solution.py:501
  17.9 1.8 %shard_map.225 = bf16[32,160,128]{2,1,0:T(8,128)(2,1)} custom-call(bf16[320,512]{1,0:T(8,128)(2,1)S(1)} %get-tuple-element.36.table_ref, s32[32,1,64]{2,1,0:T(1,128)S(1)} %all_to_all.20.wanted_ref), custom_call_target="tpu_custom_call" | custom-call | tf_op jit(solution)/shard_map/pallas_call | solution.py:561
  19.7 0.0 copy-start.10
  19.7 0.0 copy-start.11
  19.7 0.0 copy-start
  19.7 0.0 copy-start.1
  19.7 0.0 copy-start.2
  19.7 0.0 copy-start.3
  19.7 0.0 copy-start.4
  19.8 0.0 copy-start.6
  19.8 0.0 copy-start.7
  19.8 3.7 %all-to-all-start.1 = ((bf16[32,160,128]{2,1,0:T(8,128)(2,1)}), bf16[32,160,128]{2,1,0:T(8,128)(2,1)S(1)}, u32[]{:S(2)}, u32[]{:S(2)}) async-start(bf16[32,160,128]{2,1,0:T(8,128)(2,1)} %shard_map.225), calls=%async_computation.1 | async-start | bytes 2621440 | tf_op jit(solution)/shard_map/all_to_all | solution.py:487
  23.5 0.0 copy-done.10
  23.5 0.0 copy-done.11
  23.5 0.2 reshape.32
  23.7 0.1 copy.25
  23.9 4.4 %collective-permute-done.1.outer_ref = bf16[320,512]{1,0:T(8,128)(2,1)S(1)} collective-permute-done((bf16[320,512]{1,0:T(8,128)(2,1)S(1)}, bf16[320,512]{1,0:T(8,128)(2,1)S(1)}, u32[]{:S(2)}, u32[]{:S(2)}) %collective-permute-start.1) | collective-permute-done | bytes 327712 | tf_op jit(solution)/shard_map/ppermute | solution.py:501
  28.2 15.4 %collective-permute-done.inner_ref = bf16[320,512]{1,0:T(8,128)(2,1)S(1)} collective-permute-done((bf16[320,512]{1,0:T(8,128)(2,1)S(1)}, bf16[320,512]{1,0:T(8,128)(2,1)S(1)}, u32[]{:S(2)}, u32[]{:S(2)}) %collective-permute-start) | collective-permute-done | bytes 327712 | tf_op jit(solution)/shard_map/ppermute | solution.py:501
  43.7 0.0 copy-done
  43.7 0.0 copy-done.1
  43.7 0.0 copy-done.2
  43.7 0.0 copy-done.3
  43.7 0.0 copy-done.4
  43.7 0.0 copy-done.6
  43.7 0.0 copy-done.7
  43.7 0.0 copy-start.5
  43.7 0.7 copy-done.5
  44.5 0.0 copy-start.8
  44.5 0.7 copy-done.8
  45.1 0.0 copy-start.9
  45.1 0.7 copy-done.9
  45.8 9.1 %shard_map.226 = (f32[304,512]{1,0:T(8,128)}, f32[272,256]{1,0:T(8,128)}, bf16[1,384,1024]{2,1,0:T(8,128)(2,1)}, bf16[384,1024]{1,0:T(8,128)(2,1)S(1)}, s32[2,1,...) custom-call(bf16[320,512]{1,0:T(8,128)(2,1)S(1)} %get-tuple-element.36.table_ref, ...), custom_call_target="tpu_custom_call" | custom-call | flops 40000000000 | bytes 8000000 | tf_op jit(solution)/shard_map/pallas_call | solution.py:582
  54.9 1.8 %all-to-all-done.1.reply_ref = bf16[32,160,128]{2,1,0:T(8,128)(2,1)S(1)} async-done(((bf16[32,160,128]{2,1,0:T(8,128)(2,1)}), bf16[32,160,128]{2,1,0:T(8,128)(2,1)S(1)}, u32[]{:S(2)}, u32[]{:S(2)}) %all-to-all-start.1) | async-done | bytes 1310752 | tf_op jit(solution)/shard_map/all_to_all | solution.py:487
  56.7 3.5 %shard_map.227 = (bf16[304,512]{1,0:T(8,128)(2,1)S(1)}, bf16[32,5,2,128]{3,2,1,0:T(2,128)(2,1)S(1)}) custom-call(bf16[32,160,128]{2,1,0:T(8,128)(2,1)S(1)} %all-to-all-done.1.reply_ref, bf16[384,1024]{1,0:T(8,128)(2,1)S(1)} %get-tuple-element.39.first_ref, s32[2,1,1024]{2,1,0:T(1,128)S(1)} %get-tuple-element.40.code_ref, ...), custom_call_target="tpu_custom_call" | custom-call | tf_op jit(solution)/shard_map/pallas_call | solution.py:626
  60.2 9.6 %all_to_all.21.parts_ref = bf16[32,5,2,128]{3,2,1,0:T(2,128)(2,1)S(1)} all-to-all(bf16[32,5,2,128]{3,2,1,0:T(2,128)(2,1)S(1)} %get-tuple-element.46), channel_id=1, replica_groups=mesh['dom'=4,'sub'=8] {'dom','sub'}, dimensions={0} | all-to-all | bytes 163840 | tf_op jit(solution)/shard_map/all_to_all | solution.py:487
  69.8 0.1 shard_map.228
  69.9 9.1 %all_to_all.22.blocks_ref = bf16[32,5,2,128]{3,2,1,0:T(2,128)(2,1)S(1)} all-to-all(bf16[32,5,2,128]{3,2,1,0:T(2,128)(2,1)S(1)} %shard_map.228), channel_id=1, replica_groups=mesh['dom'=4,'sub'=8] {'dom','sub'}, dimensions={0} | all-to-all | bytes 163840 | tf_op jit(solution)/shard_map/all_to_all | solution.py:487
  79.0 1.1 %shard_map.229 = (bf16[304,512]{1,0:T(8,128)(2,1)}, f32[128,128]{1,0:T(8,128)}, f32[1,128]{1,0:T(1,128)}, f32[1,128]{1,0:T(1,128)}, f32[144,128]{1,0:T(8,128)}, ...) custom-call(bf16[32,5,2,128]{3,2,1,0:T(2,128)(2,1)S(1)} %all_to_all.22.blocks_ref, ...), custom_call_target="tpu_custom_call" | custom-call | tf_op jit(solution)/shard_map/pallas_call | solution.py:649
  (2 shorter events, 0.0 us)
Async XLA Ops:
  15.9 12.3 %collective-permute-start.1 = (bf16[320,512]{1,0:T(8,128)(2,1)S(1)}, bf16[320,512]{1,0:T(8,128)(2,1)S(1)}, u32[]{:S(2)}, u32[]{:S(2)}) collective-permute-start(bf16[320,512]{1,0:T(8,128)(2,1)S(1)} %get-tuple-element.36.table_ref), channel_id=1, source_target_pairs={{1,2},{3,4},{5,6},{7,0},{2,1},{4,3},{6,5},{0,7},{9,10},{11,12},{13... | collective-permute-start | bytes 983048 | tf_op jit(solution)/shard_map/ppermute | solution.py:501
  16.5 27.1 %collective-permute-start = (bf16[320,512]{1,0:T(8,128)(2,1)S(1)}, bf16[320,512]{1,0:T(8,128)(2,1)S(1)}, u32[]{:S(2)}, u32[]{:S(2)}) collective-permute-start(bf16[320,512]{1,0:T(8,128)(2,1)S(1)} %get-tuple-element.36.table_ref), channel_id=1, source_target_pairs={{0,1},{2,3},{4,5},{6,7},{1,0},{3,2},{5,4},{7,6},{8,9},{10,11},{12,... | collective-permute-start | bytes 983048 | tf_op jit(solution)/shard_map/ppermute | solution.py:501
  19.7 3.8 %copy-start.10 = (s32[3072]{0:T(1024)S(1)}, s32[3072]{0:T(1024)}, u32[]{:S(2)}) copy-start(s32[3072]{0:T(1024)} %param.20) | copy-start | bytes 36868
  19.7 3.8 %copy-start.11 = (s32[3072]{0:T(1024)S(1)}, s32[3072]{0:T(1024)}, u32[]{:S(2)}) copy-start(s32[3072]{0:T(1024)} %param.21) | copy-start | bytes 36868
  19.7 24.0 %copy-start = (bf16[304,512]{1,0:T(8,128)(2,1)S(1)}, bf16[304,512]{1,0:T(8,128)(2,1)}, u32[]{:S(2)}) copy-start(bf16[304,512]{1,0:T(8,128)(2,1)} %cot_hbm.1) | copy-start | bytes 933892
  19.7 24.0 %copy-start.1 = (bf16[64,64]{1,0:T(8,128)(2,1)S(1)}, bf16[64,64]{1,0:T(8,128)(2,1)}, u32[]{:S(2)}) copy-start(bf16[64,64]{1,0:T(8,128)(2,1)} %w_scal_ref.3) | copy-start | bytes 24580
  19.7 23.9 %copy-start.2 = (bf16[32,32]{1,0:T(8,128)(2,1)S(1)}, bf16[32,32]{1,0:T(8,128)(2,1)}, u32[]{:S(2)}) copy-start(bf16[32,32]{1,0:T(8,128)(2,1)} %w_vec_ref.3) | copy-start | bytes 6148
  19.7 23.9 %copy-start.3 = (bf16[16,16]{1,0:T(8,128)(2,1)S(1)}, bf16[16,16]{1,0:T(8,128)(2,1)}, u32[]{:S(2)}) copy-start(bf16[16,16]{1,0:T(8,128)(2,1)} %w_ten_ref.3) | copy-start | bytes 1540
  19.7 23.9 %copy-start.4 = (bf16[144,128]{1,0:T(8,128)(2,1)S(1)}, bf16[144,128]{1,0:T(8,128)(2,1)}, u32[]{:S(2)}) copy-start(bf16[144,128]{1,0:T(8,128)(2,1)} %w_two_ref.1) | copy-start | bytes 110596
  19.8 23.9 %copy-start.6 = (s32[2048]{0:T(1024)S(1)}, s32[2048]{0:T(1024)}, u32[]{:S(2)}) copy-start(s32[2048]{0:T(1024)} %param.25) | copy-start | bytes 24580
  19.8 23.9 %copy-start.7 = (s32[2048]{0:T(1024)S(1)}, s32[2048]{0:T(1024)}, u32[]{:S(2)}) copy-start(s32[2048]{0:T(1024)} %param.26) | copy-start | bytes 24580
  19.8 36.9 %all-to-all-start.1 = ((bf16[32,160,128]{2,1,0:T(8,128)(2,1)}), bf16[32,160,128]{2,1,0:T(8,128)(2,1)S(1)}, u32[]{:S(2)}, u32[]{:S(2)}) async-start(bf16[32,160,128]{2,1,0:T(8,128)(2,1)} %shard_map.225), calls=%async_computation.1 | async-start | bytes 2621440 | tf_op jit(solution)/shard_map/all_to_all | solution.py:487
  43.7 0.8 copy-start.5
  44.5 0.7 copy-start.8
  45.1 0.7 copy-start.9

commit v6 on v5

--- a/solution.py
+++ b/solution.py
@@ -19,7 +19,7 @@
 LANES = 128
 FINE = 2
 CHUNK = 512
-WIDE = 1024
+WIDE = 512
 VMEM_BYTES = 48 * 1024 * 1024
 
 

time: 80.5 us -> 81.1 us (level)
  local copies, waits for them, and re-layouts: 2.45 us -> 0.41 us
  waiting for transfers between devices: 21.6 us -> 23.5 us
    unnamed x24, local copies, waits for them, and re-layouts: 2.12 us -> 0.08 us
    all_to_all x1, waiting for transfers between devices: 1.81 us -> 3.76 us  [exchange(): return lax.all_to_all(blocks, axes, split_axis=0, concat_axis=0, tiled=True)]
where the time goes in v6:
time: 81.1 us; the launch traced here: 80.8 us
  blocking collectives  32.9 us (41%)
  waiting for transfers between devices  23.5 us (29%)
  Pallas kernels  17.4 us (21%)
  starting transfers between devices  5.69 us (7%)
  between operations  0.88 us (1%)
    all_to_all x3, blocking collectives, exchange(): return lax.all_to_all(blocks, axes, split_axis=0, concat_axis=0, tiled=True)  32.9 us
    ppermute x2, waiting for transfers between devices, swapped(): lax.ppermute(shard, axis, pairs + [(there, here) for here, there in pairs])  19.7 us
    pallas_call x1, Pallas kernels, on_device(): call(mesh_kernel, (pltpu.HBM((FEAT, node_count), f32), pltpu.HBM((mesh_ro...  9.23 us
    pallas_call x1, Pallas kernels, on_device(): call(functools.partial(contact_kernel, slot, grad_scale), (shaped((FEAT,...  4.18 us
    all_to_all x1, waiting for transfers between devices, exchange(): return lax.all_to_all(blocks, axes, split_axis=0, concat_axis=0, tiled=True)  3.76 us
    all_to_all x1, starting transfers between devices, exchange(): return lax.all_to_all(blocks, axes, split_axis=0, concat_axis=0, tiled=True)  3.7 us
    ppermute x2, starting transfers between devices, swapped(): lax.ppermute(shard, axis, pairs + [(there, here) for here, there in pairs])  1.99 us
    pallas_call x1, Pallas kernels, on_device(): call(functools.partial(contact_gather_kernel, slot), pltpu.HBM((device_co...  1.78 us
  transfers between devices with their start and end apart: 3, of which 3 were waited for; matrix products, arithmetic and copies ran while one was open for 0% of the time, Pallas kernels for 14%

profile of v6, /device:TPU:0, one launch (start us, length us, event | category | flops | bytes accessed | tf_op | source)
XLA Modules:
  0.0 80.8 jit_solution(15814827366932422419)
XLA Ops:
  0.6 1.0 %shard_map.224 = (bf16[320,512]{1,0:T(8,128)(2,1)S(1)}, s32[32,1,64]{2,1,0:T(1,128)S(1)}) custom-call(bf16[304,512]{1,0:T(8,128)(2,1)} %feat_ref.1, bf16[3,512]{1,0:T(4,128)(2,1)} %pos_ref.1, s32[1,512]{1,0:T(1,128)} %bitcast.16, s32[1,512]{1,0:T(1,128)} %bitcast.17, s32[16,128]{1,0:T(8,128)} %bitcast.15), custom_call_target="tpu_custom_call" | custom-call | tf_op jit(solution)/shard_map/pallas_call | solution.py:533
  1.7 14.2 %all_to_all.20.wanted_ref = s32[32,1,64]{2,1,0:T(1,128)S(1)} all-to-all(s32[32,1,64]{2,1,0:T(1,128)S(1)} %get-tuple-element.33), channel_id=1, replica_groups=mesh['dom'=4,'sub'=8] {'dom','sub'}, dimensions={0} | all-to-all | bytes 16384 | tf_op jit(solution)/shard_map/all_to_all | solution.py:487
  15.9 0.6 collective-permute-start.1
  16.5 1.4 %collective-permute-start = (bf16[320,512]{1,0:T(8,128)(2,1)S(1)}, bf16[320,512]{1,0:T(8,128)(2,1)S(1)}, u32[]{:S(2)}, u32[]{:S(2)}) collective-permute-start(bf16[320,512]{1,0:T(8,128)(2,1)S(1)} %get-tuple-element.36.table_ref), channel_id=1, source_target_pairs={{0,1},{2,3},{4,5},{6,7},{1,0},{3,2},{5,4},{7,6},{8,9},{10,11},{12,... | collective-permute-start | bytes 983048 | tf_op jit(solution)/shard_map/ppermute | solution.py:501
  17.9 1.8 %shard_map.225 = bf16[32,160,128]{2,1,0:T(8,128)(2,1)} custom-call(bf16[320,512]{1,0:T(8,128)(2,1)S(1)} %get-tuple-element.36.table_ref, s32[32,1,64]{2,1,0:T(1,128)S(1)} %all_to_all.20.wanted_ref), custom_call_target="tpu_custom_call" | custom-call | tf_op jit(solution)/shard_map/pallas_call | solution.py:561
  19.7 0.0 copy-start.10
  19.7 0.0 copy-start.11
  19.7 0.0 copy-start
  19.7 0.0 copy-start.1
  19.7 0.0 copy-start.2
  19.7 0.0 copy-start.3
  19.7 0.0 copy-start.4
  19.8 0.0 copy-start.5
  19.8 0.0 copy-start.6
  19.8 0.0 copy-start.7
  19.8 0.0 copy-start.8
  19.8 0.0 copy-start.9
  19.8 3.7 %all-to-all-start.1 = ((bf16[32,160,128]{2,1,0:T(8,128)(2,1)}), bf16[32,160,128]{2,1,0:T(8,128)(2,1)S(1)}, u32[]{:S(2)}, u32[]{:S(2)}) async-start(bf16[32,160,128]{2,1,0:T(8,128)(2,1)} %shard_map.225), calls=%async_computation.1 | async-start | bytes 2621440 | tf_op jit(solution)/shard_map/all_to_all | solution.py:487
  23.5 0.0 copy-done.10
  23.5 0.0 copy-done.11
  23.6 0.2 reshape.32
  23.8 0.1 copy.25
  23.9 4.3 %collective-permute-done.1.outer_ref = bf16[320,512]{1,0:T(8,128)(2,1)S(1)} collective-permute-done((bf16[320,512]{1,0:T(8,128)(2,1)S(1)}, bf16[320,512]{1,0:T(8,128)(2,1)S(1)}, u32[]{:S(2)}, u32[]{:S(2)}) %collective-permute-start.1) | collective-permute-done | bytes 327712 | tf_op jit(solution)/shard_map/ppermute | solution.py:501
  28.2 15.4 %collective-permute-done.inner_ref = bf16[320,512]{1,0:T(8,128)(2,1)S(1)} collective-permute-done((bf16[320,512]{1,0:T(8,128)(2,1)S(1)}, bf16[320,512]{1,0:T(8,128)(2,1)S(1)}, u32[]{:S(2)}, u32[]{:S(2)}) %collective-permute-start) | collective-permute-done | bytes 327712 | tf_op jit(solution)/shard_map/ppermute | solution.py:501
  43.7 0.0 copy-done
  43.7 0.0 copy-done.1
  43.7 0.0 copy-done.2
  43.7 0.0 copy-done.3
  43.7 0.0 copy-done.4
  43.7 0.0 copy-done.5
  43.7 0.0 copy-done.6
  43.7 0.0 copy-done.7
  43.7 0.0 copy-done.8
  43.7 0.0 copy-done.9
  43.7 9.2 %shard_map.226 = (f32[304,512]{1,0:T(8,128)}, f32[272,256]{1,0:T(8,128)}, bf16[3,384,512]{2,1,0:T(8,128)(2,1)}, bf16[384,512]{1,0:T(8,128)(2,1)S(1)}, s32[4,1,51...) custom-call(bf16[320,512]{1,0:T(8,128)(2,1)S(1)} %get-tuple-element.36.table_ref, ...), custom_call_target="tpu_custom_call" | custom-call | flops 40000000000 | bytes 8000000 | tf_op jit(solution)/shard_map/pallas_call | solution.py:582
  53.0 3.8 %all-to-all-done.1.reply_ref = bf16[32,160,128]{2,1,0:T(8,128)(2,1)S(1)} async-done(((bf16[32,160,128]{2,1,0:T(8,128)(2,1)}), bf16[32,160,128]{2,1,0:T(8,128)(2,1)S(1)}, u32[]{:S(2)}, u32[]{:S(2)}) %all-to-all-start.1) | async-done | bytes 1310752 | tf_op jit(solution)/shard_map/all_to_all | solution.py:487
  56.7 4.2 %shard_map.227 = (bf16[304,512]{1,0:T(8,128)(2,1)S(1)}, bf16[32,5,2,128]{3,2,1,0:T(2,128)(2,1)S(1)}) custom-call(bf16[32,160,128]{2,1,0:T(8,128)(2,1)S(1)} %all-to-all-done.1.reply_ref, bf16[384,512]{1,0:T(8,128)(2,1)S(1)} %get-tuple-element.39.first_ref, s32[4,1,512]{2,1,0:T(1,128)S(1)} %get-tuple-element.40.code_ref, ...), custom_call_target="tpu_custom_call" | custom-call | tf_op jit(solution)/shard_map/pallas_call | solution.py:626
  60.9 9.6 %all_to_all.21.parts_ref = bf16[32,5,2,128]{3,2,1,0:T(2,128)(2,1)S(1)} all-to-all(bf16[32,5,2,128]{3,2,1,0:T(2,128)(2,1)S(1)} %get-tuple-element.46), channel_id=1, replica_groups=mesh['dom'=4,'sub'=8] {'dom','sub'}, dimensions={0} | all-to-all | bytes 163840 | tf_op jit(solution)/shard_map/all_to_all | solution.py:487
  70.5 0.1 shard_map.228
  70.6 9.1 %all_to_all.22.blocks_ref = bf16[32,5,2,128]{3,2,1,0:T(2,128)(2,1)S(1)} all-to-all(bf16[32,5,2,128]{3,2,1,0:T(2,128)(2,1)S(1)} %shard_map.228), channel_id=1, replica_groups=mesh['dom'=4,'sub'=8] {'dom','sub'}, dimensions={0} | all-to-all | bytes 163840 | tf_op jit(solution)/shard_map/all_to_all | solution.py:487
  79.7 1.1 %shard_map.229 = (bf16[304,512]{1,0:T(8,128)(2,1)}, f32[128,128]{1,0:T(8,128)}, f32[1,128]{1,0:T(1,128)}, f32[1,128]{1,0:T(1,128)}, f32[144,128]{1,0:T(8,128)}, ...) custom-call(bf16[32,5,2,128]{3,2,1,0:T(2,128)(2,1)S(1)} %all_to_all.22.blocks_ref, ...), custom_call_target="tpu_custom_call" | custom-call | tf_op jit(solution)/shard_map/pallas_call | solution.py:649
  (2 shorter events, 0.0 us)
Async XLA Ops:
  15.9 12.3 %collective-permute-start.1 = (bf16[320,512]{1,0:T(8,128)(2,1)S(1)}, bf16[320,512]{1,0:T(8,128)(2,1)S(1)}, u32[]{:S(2)}, u32[]{:S(2)}) collective-permute-start(bf16[320,512]{1,0:T(8,128)(2,1)S(1)} %get-tuple-element.36.table_ref), channel_id=1, source_target_pairs={{1,2},{3,4},{5,6},{7,0},{2,1},{4,3},{6,5},{0,7},{9,10},{11,12},{13... | collective-permute-start | bytes 983048 | tf_op jit(solution)/shard_map/ppermute | solution.py:501
  16.5 27.1 %collective-permute-start = (bf16[320,512]{1,0:T(8,128)(2,1)S(1)}, bf16[320,512]{1,0:T(8,128)(2,1)S(1)}, u32[]{:S(2)}, u32[]{:S(2)}) collective-permute-start(bf16[320,512]{1,0:T(8,128)(2,1)S(1)} %get-tuple-element.36.table_ref), channel_id=1, source_target_pairs={{0,1},{2,3},{4,5},{6,7},{1,0},{3,2},{5,4},{7,6},{8,9},{10,11},{12,... | collective-permute-start | bytes 983048 | tf_op jit(solution)/shard_map/ppermute | solution.py:501
  19.7 3.9 %copy-start.10 = (s32[3072]{0:T(1024)S(1)}, s32[3072]{0:T(1024)}, u32[]{:S(2)}) copy-start(s32[3072]{0:T(1024)} %param.20) | copy-start | bytes 36868
  19.7 3.9 %copy-start.11 = (s32[3072]{0:T(1024)S(1)}, s32[3072]{0:T(1024)}, u32[]{:S(2)}) copy-start(s32[3072]{0:T(1024)} %param.21) | copy-start | bytes 36868
  19.7 24.0 %copy-start = (bf16[304,512]{1,0:T(8,128)(2,1)S(1)}, bf16[304,512]{1,0:T(8,128)(2,1)}, u32[]{:S(2)}) copy-start(bf16[304,512]{1,0:T(8,128)(2,1)} %cot_hbm.1) | copy-start | bytes 933892
  19.7 24.0 %copy-start.1 = (bf16[64,64]{1,0:T(8,128)(2,1)S(1)}, bf16[64,64]{1,0:T(8,128)(2,1)}, u32[]{:S(2)}) copy-start(bf16[64,64]{1,0:T(8,128)(2,1)} %w_scal_ref.3) | copy-start | bytes 24580
  19.7 23.9 %copy-start.2 = (bf16[32,32]{1,0:T(8,128)(2,1)S(1)}, bf16[32,32]{1,0:T(8,128)(2,1)}, u32[]{:S(2)}) copy-start(bf16[32,32]{1,0:T(8,128)(2,1)} %w_vec_ref.3) | copy-start | bytes 6148
  19.7 23.9 %copy-start.3 = (bf16[16,16]{1,0:T(8,128)(2,1)S(1)}, bf16[16,16]{1,0:T(8,128)(2,1)}, u32[]{:S(2)}) copy-start(bf16[16,16]{1,0:T(8,128)(2,1)} %w_ten_ref.3) | copy-start | bytes 1540
  19.7 23.9 %copy-start.4 = (bf16[144,128]{1,0:T(8,128)(2,1)S(1)}, bf16[144,128]{1,0:T(8,128)(2,1)}, u32[]{:S(2)}) copy-start(bf16[144,128]{1,0:T(8,128)(2,1)} %w_two_ref.1) | copy-start | bytes 110596
  19.8 23.9 %copy-start.5 = (bf16[128,128]{1,0:T(8,128)(2,1)S(1)}, bf16[128,128]{1,0:T(8,128)(2,1)}, u32[]{:S(2)}) copy-start(bf16[128,128]{1,0:T(8,128)(2,1)} %w_one_ref.1) | copy-start | bytes 98308
  19.8 23.9 %copy-start.6 = (s32[2048]{0:T(1024)S(1)}, s32[2048]{0:T(1024)}, u32[]{:S(2)}) copy-start(s32[2048]{0:T(1024)} %param.25) | copy-start | bytes 24580
  19.8 23.9 %copy-start.7 = (s32[2048]{0:T(1024)S(1)}, s32[2048]{0:T(1024)}, u32[]{:S(2)}) copy-start(s32[2048]{0:T(1024)} %param.26) | copy-start | bytes 24580
  19.8 23.9 %copy-start.8 = (f32[128]{0:T(128)S(1)}, f32[128]{0:T(128)}, u32[]{:S(2)}) copy-start(f32[128]{0:T(128)} %param.28) | copy-start | bytes 1540
  19.8 23.9 %copy-start.9 = (f32[128]{0:T(128)S(1)}, f32[128]{0:T(128)}, u32[]{:S(2)}) copy-start(f32[128]{0:T(128)} %param.29) | copy-start | bytes 1540
  19.8 36.9 %all-to-all-start.1 = ((bf16[32,160,128]{2,1,0:T(8,128)(2,1)}), bf16[32,160,128]{2,1,0:T(8,128)(2,1)S(1)}, u32[]{:S(2)}, u32[]{:S(2)}) async-start(bf16[32,160,128]{2,1,0:T(8,128)(2,1)} %shard_map.225), calls=%async_computation.1 | async-start | bytes 2621440 | tf_op jit(solution)/shard_map/all_to_all | solution.py:487

commit v7 on v3

--- a/solution.py
+++ b/solution.py
@@ -327,8 +327,7 @@
     for chunk in range(chunks):
         src_rows = src_scr[chunk]
         if chunk == 1:
-            for copy in copies:
-                copy.wait()
+            copies[0].wait()
         recv = first_ref[...] if chunk == 0 else recv_ref[chunk - 1]
         inputs = jnp.concatenate([recv[FEAT + 16 :], src_rows[:CS]], 0)
         message, grads = edge_math(
@@ -342,15 +341,14 @@
             weights,
         )
         scattered = dot(message.astype(jnp.bfloat16), one_hot(code_ref[chunk], node_count), 1, 1)
-        if chunk == 0:
-            held = (scattered, grads)
-            continue
-        agg_ref[...] += scattered
-        add_grads(grads_ref, grads)
-        if chunk == 1:
-            agg_ref[...] += held[0]
-            add_grads(grads_ref, held[1])
-    agg_rows = agg_ref[...].astype(jnp.bfloat16)
+        if chunk > 0:
+            scattered = held[0] + scattered
+            grads = [before + now for before, now in zip(held[1], grads)]
+        held = (scattered, grads)
+    for copy in copies[1:]:
+        copy.wait()
+    add_grads(grads_ref, held[1])
+    agg_rows = (agg_ref[...] + held[0]).astype(jnp.bfloat16)
     agg_out_ref[...] = agg_rows
     cot = cot_ref[...]
     low = HID + GATES

time: 80.5 us -> 80.4 us (level)
  no operation moved by 1% of the time
where the time goes in v7:
time: 80.4 us; the launch traced here: 80 us
  blocking collectives  32.9 us (41%)
  waiting for transfers between devices  21.6 us (27%)
  Pallas kernels  16.5 us (21%)
  starting transfers between devices  5.69 us (7%)
  local copies, waits for them, and re-layouts  2.45 us (3%)
  between operations  0.84 us (1%)
    all_to_all x3, blocking collectives, exchange(): return lax.all_to_all(blocks, axes, split_axis=0, concat_axis=0, tiled=True)  32.9 us
    ppermute x2, waiting for transfers between devices, swapped(): lax.ppermute(shard, axis, pairs + [(there, here) for here, there in pairs])  19.8 us
    pallas_call x1, Pallas kernels, on_device(): call(mesh_kernel, (pltpu.HBM((FEAT, node_count), f32), pltpu.HBM((mesh_ro...  9.09 us
    all_to_all x1, starting transfers between devices, exchange(): return lax.all_to_all(blocks, axes, split_axis=0, concat_axis=0, tiled=True)  3.7 us
    pallas_call x1, Pallas kernels, on_device(): call(functools.partial(contact_kernel, slot, grad_scale), (shaped((FEAT,...  3.42 us
    unnamed x24, local copies, waits for them, and re-layouts  2.12 us
    ppermute x2, starting transfers between devices, swapped(): lax.ppermute(shard, axis, pairs + [(there, here) for here, there in pairs])  1.99 us
    all_to_all x1, waiting for transfers between devices, exchange(): return lax.all_to_all(blocks, axes, split_axis=0, concat_axis=0, tiled=True)  1.81 us
  transfers between devices with their start and end apart: 3, of which 3 were waited for; matrix products, arithmetic and copies ran while one was open for 0% of the time, Pallas kernels for 14%

profile of v7, /device:TPU:0, one launch (start us, length us, event | category | flops | bytes accessed | tf_op | source)
XLA Modules:
  0.0 80.0 jit_solution(2499463058797471396)
XLA Ops:
  0.6 1.0 %shard_map.224 = (bf16[320,512]{1,0:T(8,128)(2,1)S(1)}, s32[32,1,64]{2,1,0:T(1,128)S(1)}) custom-call(bf16[304,512]{1,0:T(8,128)(2,1)} %feat_ref.1, bf16[3,512]{1,0:T(4,128)(2,1)} %pos_ref.1, s32[1,512]{1,0:T(1,128)} %bitcast.16, s32[1,512]{1,0:T(1,128)} %bitcast.17, s32[16,128]{1,0:T(8,128)} %bitcast.15), custom_call_target="tpu_custom_call" | custom-call | tf_op jit(solution)/shard_map/pallas_call | solution.py:521
  1.7 14.2 %all_to_all.20.wanted_ref = s32[32,1,64]{2,1,0:T(1,128)S(1)} all-to-all(s32[32,1,64]{2,1,0:T(1,128)S(1)} %get-tuple-element.33), channel_id=1, replica_groups=mesh['dom'=4,'sub'=8] {'dom','sub'}, dimensions={0} | all-to-all | bytes 16384 | tf_op jit(solution)/shard_map/all_to_all | solution.py:475
  15.9 0.6 collective-permute-start.1
  16.5 1.4 %collective-permute-start = (bf16[320,512]{1,0:T(8,128)(2,1)S(1)}, bf16[320,512]{1,0:T(8,128)(2,1)S(1)}, u32[]{:S(2)}, u32[]{:S(2)}) collective-permute-start(bf16[320,512]{1,0:T(8,128)(2,1)S(1)} %get-tuple-element.36.table_ref), channel_id=1, source_target_pairs={{0,1},{2,3},{4,5},{6,7},{1,0},{3,2},{5,4},{7,6},{8,9},{10,11},{12,... | collective-permute-start | bytes 983048 | tf_op jit(solution)/shard_map/ppermute | solution.py:489
  17.9 1.8 %shard_map.225 = bf16[32,160,128]{2,1,0:T(8,128)(2,1)} custom-call(bf16[320,512]{1,0:T(8,128)(2,1)S(1)} %get-tuple-element.36.table_ref, s32[32,1,64]{2,1,0:T(1,128)S(1)} %all_to_all.20.wanted_ref), custom_call_target="tpu_custom_call" | custom-call | tf_op jit(solution)/shard_map/pallas_call | solution.py:549
  19.7 0.0 copy-start.10
  19.7 0.0 copy-start.11
  19.7 0.0 copy-start
  19.7 0.0 copy-start.1
  19.7 0.0 copy-start.2
  19.7 0.0 copy-start.3
  19.7 0.0 copy-start.4
  19.8 0.0 copy-start.6
  19.8 0.0 copy-start.7
  19.8 3.7 %all-to-all-start.1 = ((bf16[32,160,128]{2,1,0:T(8,128)(2,1)}), bf16[32,160,128]{2,1,0:T(8,128)(2,1)S(1)}, u32[]{:S(2)}, u32[]{:S(2)}) async-start(bf16[32,160,128]{2,1,0:T(8,128)(2,1)} %shard_map.225), calls=%async_computation.1 | async-start | bytes 2621440 | tf_op jit(solution)/shard_map/all_to_all | solution.py:475
  23.5 0.0 copy-done.10
  23.5 0.0 copy-done.11
  23.5 0.2 reshape.32
  23.7 0.1 copy.25
  23.9 4.4 %collective-permute-done.1.outer_ref = bf16[320,512]{1,0:T(8,128)(2,1)S(1)} collective-permute-done((bf16[320,512]{1,0:T(8,128)(2,1)S(1)}, bf16[320,512]{1,0:T(8,128)(2,1)S(1)}, u32[]{:S(2)}, u32[]{:S(2)}) %collective-permute-start.1) | collective-permute-done | bytes 327712 | tf_op jit(solution)/shard_map/ppermute | solution.py:489
  28.2 15.4 %collective-permute-done.inner_ref = bf16[320,512]{1,0:T(8,128)(2,1)S(1)} collective-permute-done((bf16[320,512]{1,0:T(8,128)(2,1)S(1)}, bf16[320,512]{1,0:T(8,128)(2,1)S(1)}, u32[]{:S(2)}, u32[]{:S(2)}) %collective-permute-start) | collective-permute-done | bytes 327712 | tf_op jit(solution)/shard_map/ppermute | solution.py:489
  43.7 0.0 copy-done
  43.7 0.0 copy-done.1
  43.7 0.0 copy-done.2
  43.7 0.0 copy-done.3
  43.7 0.0 copy-done.4
  43.7 0.0 copy-done.6
  43.7 0.0 copy-done.7
  43.7 0.0 copy-start.5
  43.7 0.7 copy-done.5
  44.5 0.0 copy-start.8
  44.5 0.7 copy-done.8
  45.1 0.0 copy-start.9
  45.1 0.7 copy-done.9
  45.8 9.1 %shard_map.226 = (f32[304,512]{1,0:T(8,128)}, f32[272,256]{1,0:T(8,128)}, bf16[1,384,1024]{2,1,0:T(8,128)(2,1)}, bf16[384,1024]{1,0:T(8,128)(2,1)S(1)}, s32[2,1,...) custom-call(bf16[320,512]{1,0:T(8,128)(2,1)S(1)} %get-tuple-element.36.table_ref, ...), custom_call_target="tpu_custom_call" | custom-call | flops 40000000000 | bytes 8000000 | tf_op jit(solution)/shard_map/pallas_call | solution.py:570
  54.9 1.8 %all-to-all-done.1.reply_ref = bf16[32,160,128]{2,1,0:T(8,128)(2,1)S(1)} async-done(((bf16[32,160,128]{2,1,0:T(8,128)(2,1)}), bf16[32,160,128]{2,1,0:T(8,128)(2,1)S(1)}, u32[]{:S(2)}, u32[]{:S(2)}) %all-to-all-start.1) | async-done | bytes 1310752 | tf_op jit(solution)/shard_map/all_to_all | solution.py:475
  56.7 3.4 %shard_map.227 = (bf16[304,512]{1,0:T(8,128)(2,1)S(1)}, bf16[32,5,2,128]{3,2,1,0:T(2,128)(2,1)S(1)}) custom-call(bf16[32,160,128]{2,1,0:T(8,128)(2,1)S(1)} %all-to-all-done.1.reply_ref, bf16[384,1024]{1,0:T(8,128)(2,1)S(1)} %get-tuple-element.39.first_ref, s32[2,1,1024]{2,1,0:T(1,128)S(1)} %get-tuple-element.40.code_ref, ...), custom_call_target="tpu_custom_call" | custom-call | tf_op jit(solution)/shard_map/pallas_call | solution.py:614
  60.1 9.6 %all_to_all.21.parts_ref = bf16[32,5,2,128]{3,2,1,0:T(2,128)(2,1)S(1)} all-to-all(bf16[32,5,2,128]{3,2,1,0:T(2,128)(2,1)S(1)} %get-tuple-element.46), channel_id=1, replica_groups=mesh['dom'=4,'sub'=8] {'dom','sub'}, dimensions={0} | all-to-all | bytes 163840 | tf_op jit(solution)/shard_map/all_to_all | solution.py:475
  69.7 0.1 shard_map.228
  69.8 9.1 %all_to_all.22.blocks_ref = bf16[32,5,2,128]{3,2,1,0:T(2,128)(2,1)S(1)} all-to-all(bf16[32,5,2,128]{3,2,1,0:T(2,128)(2,1)S(1)} %shard_map.228), channel_id=1, replica_groups=mesh['dom'=4,'sub'=8] {'dom','sub'}, dimensions={0} | all-to-all | bytes 163840 | tf_op jit(solution)/shard_map/all_to_all | solution.py:475
  78.9 1.1 %shard_map.229 = (bf16[304,512]{1,0:T(8,128)(2,1)}, f32[128,128]{1,0:T(8,128)}, f32[1,128]{1,0:T(1,128)}, f32[1,128]{1,0:T(1,128)}, f32[144,128]{1,0:T(8,128)}, ...) custom-call(bf16[32,5,2,128]{3,2,1,0:T(2,128)(2,1)S(1)} %all_to_all.22.blocks_ref, ...), custom_call_target="tpu_custom_call" | custom-call | tf_op jit(solution)/shard_map/pallas_call | solution.py:637
  (2 shorter events, 0.0 us)
Async XLA Ops:
  15.9 12.3 %collective-permute-start.1 = (bf16[320,512]{1,0:T(8,128)(2,1)S(1)}, bf16[320,512]{1,0:T(8,128)(2,1)S(1)}, u32[]{:S(2)}, u32[]{:S(2)}) collective-permute-start(bf16[320,512]{1,0:T(8,128)(2,1)S(1)} %get-tuple-element.36.table_ref), channel_id=1, source_target_pairs={{1,2},{3,4},{5,6},{7,0},{2,1},{4,3},{6,5},{0,7},{9,10},{11,12},{13... | collective-permute-start | bytes 983048 | tf_op jit(solution)/shard_map/ppermute | solution.py:489
  16.5 27.1 %collective-permute-start = (bf16[320,512]{1,0:T(8,128)(2,1)S(1)}, bf16[320,512]{1,0:T(8,128)(2,1)S(1)}, u32[]{:S(2)}, u32[]{:S(2)}) collective-permute-start(bf16[320,512]{1,0:T(8,128)(2,1)S(1)} %get-tuple-element.36.table_ref), channel_id=1, source_target_pairs={{0,1},{2,3},{4,5},{6,7},{1,0},{3,2},{5,4},{7,6},{8,9},{10,11},{12,... | collective-permute-start | bytes 983048 | tf_op jit(solution)/shard_map/ppermute | solution.py:489
  19.7 3.8 %copy-start.10 = (s32[3072]{0:T(1024)S(1)}, s32[3072]{0:T(1024)}, u32[]{:S(2)}) copy-start(s32[3072]{0:T(1024)} %param.20) | copy-start | bytes 36868
  19.7 3.8 %copy-start.11 = (s32[3072]{0:T(1024)S(1)}, s32[3072]{0:T(1024)}, u32[]{:S(2)}) copy-start(s32[3072]{0:T(1024)} %param.21) | copy-start | bytes 36868
  19.7 24.0 %copy-start = (bf16[304,512]{1,0:T(8,128)(2,1)S(1)}, bf16[304,512]{1,0:T(8,128)(2,1)}, u32[]{:S(2)}) copy-start(bf16[304,512]{1,0:T(8,128)(2,1)} %cot_hbm.1) | copy-start | bytes 933892
  19.7 24.0 %copy-start.1 = (bf16[64,64]{1,0:T(8,128)(2,1)S(1)}, bf16[64,64]{1,0:T(8,128)(2,1)}, u32[]{:S(2)}) copy-start(bf16[64,64]{1,0:T(8,128)(2,1)} %w_scal_ref.3) | copy-start | bytes 24580
  19.7 23.9 %copy-start.2 = (bf16[32,32]{1,0:T(8,128)(2,1)S(1)}, bf16[32,32]{1,0:T(8,128)(2,1)}, u32[]{:S(2)}) copy-start(bf16[32,32]{1,0:T(8,128)(2,1)} %w_vec_ref.3) | copy-start | bytes 6148
  19.7 23.9 %copy-start.3 = (bf16[16,16]{1,0:T(8,128)(2,1)S(1)}, bf16[16,16]{1,0:T(8,128)(2,1)}, u32[]{:S(2)}) copy-start(bf16[16,16]{1,0:T(8,128)(2,1)} %w_ten_ref.3) | copy-start | bytes 1540
  19.7 23.9 %copy-start.4 = (bf16[144,128]{1,0:T(8,128)(2,1)S(1)}, bf16[144,128]{1,0:T(8,128)(2,1)}, u32[]{:S(2)}) copy-start(bf16[144,128]{1,0:T(8,128)(2,1)} %w_two_ref.1) | copy-start | bytes 110596
  19.8 23.9 %copy-start.6 = (s32[2048]{0:T(1024)S(1)}, s32[2048]{0:T(1024)}, u32[]{:S(2)}) copy-start(s32[2048]{0:T(1024)} %param.25) | copy-start | bytes 24580
  19.8 23.9 %copy-start.7 = (s32[2048]{0:T(1024)S(1)}, s32[2048]{0:T(1024)}, u32[]{:S(2)}) copy-start(s32[2048]{0:T(1024)} %param.26) | copy-start | bytes 24580
  19.8 36.9 %all-to-all-start.1 = ((bf16[32,160,128]{2,1,0:T(8,128)(2,1)}), bf16[32,160,128]{2,1,0:T(8,128)(2,1)S(1)}, u32[]{:S(2)}, u32[]{:S(2)}) async-start(bf16[32,160,128]{2,1,0:T(8,128)(2,1)} %shard_map.225), calls=%async_computation.1 | async-start | bytes 2621440 | tf_op jit(solution)/shard_map/all_to_all | solution.py:475
  43.7 0.8 copy-start.5
  44.5 0.7 copy-start.8
  45.1 0.7 copy-start.9
